TPU v7x, 768 devices: a whole 4x8x12 slice. The times are simulated.
768 devices in a mesh: region: 12 (over z), group: 64 (over y, x, core).
Axes of the slice: x: 4, y: 8, z: 12, core: 2. Of those that a mesh axis runs over, the one named last changes fastest.
Arguments:
- coeffs: float32 [1536, 24576], P('group', 'region'), may hold values from -6 to 6
- region_of: int32 [24576, 1], P('region'), may hold values from 0 to 11; in each aligned block of 2048 rows (0 to 2047, 2048 to 4095, ...) at most 512 rows name the same one
- block_pairs: int32 [12, 64, 2], P('region'), may hold values from 0 to 47, as said below
- block_owner: int32 [12, 64], P('region'), may hold values from 0 to 63, each once within a row
Outputs:
- corrected: float32 [1536, 24576], P('group', 'region')
- margin_blocks: float32 [12, 64, 128, 128], P('region', 'group')
Inputs may be any that keep to these rules, and one draw needn't show every extreme that they name: `region_of`: among the 2048 functions of one index of region at most 512 name the same region, and that many do in every draw. `block_pairs`: for each region 64 distinct pairs (I, J) of its 48 blocks with I <= J; all 48 pairs (I, I) are among them. `block_owner`: each region's row names every position once; index g of group holds positions g * 1 to (g + 1) - 1.
All inputs are finite; a program needn't handle non-finite values.
Results may differ from a plain program's by a relative error of at most 0.0003.
Values sent between devices are 32-bit elements; how exact they have to be, the bound alone decides.
A program may use at most 32 MiB of HBM per device.

v0:
```python
import jax
import jax.numpy as jnp
from jax import lax
from jax.sharding import PartitionSpec as P

COEFFICIENT_SIZE = 1536
FB = 128
BPS = 4


def slot_index(target, region_count, step_offset):
    onehot = (target[:, None] == jnp.arange(region_count, dtype=jnp.int32)[None, :]).astype(
        jnp.int32
    )
    rank_in = jnp.sum((jnp.cumsum(onehot, axis=0) - onehot) * onehot, axis=1)
    return target * step_offset + rank_in


def margin_of(regional, pair_list):
    left_cols = regional[:, pair_list[:, 0]]
    right_cols = regional[:, pair_list[:, 1]]
    return jnp.einsum("ckf,ckg->kfg", left_cols, right_cols, precision=lax.Precision.HIGHEST)


def change_of(regional, pair_list, blocks):
    left_idx = pair_list[:, 0]
    right_idx = pair_list[:, 1]
    on_diag = (left_idx == right_idx).astype(jnp.float32)
    identity = jnp.eye(blocks.shape[1], dtype=jnp.float32)
    shifted = blocks - identity[None] * on_diag[:, None, None]
    toward_leftward = jnp.einsum(
        "ckg,kfg->ckf", regional[:, right_idx], shifted, precision=lax.Precision.HIGHEST
    )
    to_right = jnp.einsum(
        "ckf,kfg->ckg", regional[:, left_idx], shifted, precision=lax.Precision.HIGHEST
    )
    to_right = to_right * (1.0 - on_diag)[None, :, None]
    block_count = regional.shape[1]
    numbers = jnp.arange(block_count, dtype=jnp.int32)[None, :]
    onehot_leftward = (left_idx[:, None] == numbers).astype(jnp.float32)
    hot_right = (right_idx[:, None] == numbers).astype(jnp.float32)
    leading_portion = jnp.einsum(
        "atw,td->adw", toward_leftward, onehot_leftward, precision=lax.Precision.HIGHEST
    )
    second_part = jnp.einsum("ckg,kb->cbg", to_right, hot_right, precision=lax.Precision.HIGHEST)
    return leading_portion + second_part


def body(coeffs, region_of, block_pairs, block_owner):
    coef_rows = coeffs.shape[0]
    region_count = lax.axis_size("region")
    step_offset = BPS * FB
    slot_count = region_count * step_offset
    targets = region_of[:, 0]
    slot_of = slot_index(targets, region_count, step_offset)
    outgoing = jnp.zeros((coef_rows, slot_count), coeffs.dtype).at[:, slot_of].set(coeffs)
    incoming = lax.all_to_all(outgoing, "region", split_axis=1, concat_axis=1, tiled=True)
    regional = incoming.reshape(coef_rows, region_count * BPS, FB)
    pair_list = block_pairs[0]
    owners = block_owner[0]
    pair_count = pair_list.shape[0]
    by_owner = (
        jnp.zeros((pair_count,), jnp.int32).at[owners].set(jnp.arange(pair_count, dtype=jnp.int32))
    )
    ordered = pair_list[by_owner]
    partial_sums = margin_of(regional, ordered)
    owned_block = (
        lax.psum_scatter(partial_sums, "group", scatter_dimension=0, tiled=True) / COEFFICIENT_SIZE
    )
    every_block = lax.all_gather(owned_block, "group", axis=0, tiled=True)
    change = change_of(regional, ordered, every_block)
    updated = (regional - 0.5 * change).reshape(coef_rows, slot_count)
    handed_result = lax.all_to_all(updated, "region", split_axis=1, concat_axis=1, tiled=True)
    return (handed_result[:, slot_of], owned_block[None])


def solution(mesh):
    placed = (P("group", "region"), P("region", None), P("region", None, None), P("region", None))
    return jax.shard_map(
        body,
        mesh=mesh,
        in_specs=placed,
        out_specs=(P("group", "region"), P("region", "group", None, None)),
        check_vma=False,
    )
```

profile of v0, /device:TPU:1, one launch (start us, length us, event | category | flops | bytes accessed | tf_op | source)
XLA Modules:
  0.0 392.9 jit_solution(10960814254531855483)
XLA Ops:
  7.2 0.7 fusion.24
  7.9 3.4 reduce-window.6
  11.3 0.4 slice_reduce_fusion
  11.6 0.2 reduce-window.9
  11.8 0.1 broadcast_add_fusion
  12.0 0.7 fusion.23
  12.7 0.7 compare_select_fusion.3
  13.4 2.3 copy.26
  15.7 0.0 copy-start.1
  15.7 0.0 copy-start.2
  15.7 6.7 %scatter_custom_fusion = f32[24,6144]{0,1:T(8,128)S(1)} fusion(s32[2048]{0:T(1024)S(1)} %bitcast.58, f32[2048,24]{1,0:T(8,128)} %copy.26, f32[]{:T(128)} %constant.9.clone.1), kind=kCustom, calls=%fused_computation.13 | custom fusion | bytes 590336 | tf_op jit(solution)/shard_map/scatter | solution.py:56
  22.4 1.8 copy.27
  24.3 15.7 %all-to-all-start = ((f32[24,12,512]{2,0,1:T(8,128)}), f32[24,12,512]{2,0,1:T(8,128)S(1)}, u32[]{:S(2)}, u32[]{:S(2)}) async-start(f32[24,12,512]{2,0,1:T(8,128)} %copy.27), calls=%async_computation | async-start | bytes 1179648 | tf_op jit(solution)/shard_map/all_to_all | solution.py:57
  40.0 0.0 reduce-scatter.4.cloned.1.call-start
  40.0 0.0 copy-done.1
  40.0 0.1 copy.32
  40.1 0.0 copy-done.2
  40.1 0.1 copy.29
  40.2 0.1 fusion.26
  40.4 0.8 scatter_custom_fusion.1
  41.2 0.6 gather_fusion
  41.8 0.2 slice_reduce_fusion.1
  42.0 21.2 %all-to-all-done = f32[24,12,512]{2,0,1:T(8,128)S(1)} async-done(((f32[24,12,512]{2,0,1:T(8,128)}), f32[24,12,512]{2,0,1:T(8,128)S(1)}, u32[]{:S(2)}, u32[]{:S(2)}) %all-to-all-start) | async-done | bytes 589856 | tf_op jit(solution)/shard_map/all_to_all | solution.py:57
  63.2 0.4 copy.28
  63.6 0.1 reshape.89
  63.6 0.2 copy.33
  63.8 0.6 gather_fusion.2
  64.5 0.6 gather_fusion.1
  65.1 8.2 %fusion.14 = f32[64,128,128]{2,1,0:T(8,128)} fusion(f32[64,24,128]{2,1,0:T(8,128)S(1)} %gather_fusion.2, f32[64,24,128]{2,1,0:T(8,128)S(1)} %gather_fusion.1), kind=kOutput, calls=%fused_computation.22 | convolution fusion | flops 301989888 | bytes 5767168 | tf_op jit(solution)/shard_map/ckf,ckg->kfg/dot_general | solution.py:22
  73.3 0.0 reduce-scatter.4.cloned.1.call-update
  73.3 0.2 all-gather.2.cloned.1.call-start
  73.6 153.2 %reduce-scatter.4.cloned.1.call-done = f32[1,128,128]{2,1,0:T(8,128)} async-done(((f32[64,128,128]{2,1,0:T(8,128)}), f32[1,128,128]{2,1,0:T(8,128)}) %reduce-scatter.4.cloned.1.call-update) | async-done | bytes 65552
  226.7 1.5 fusion.37
  228.2 0.0 all-gather.2.cloned.1.call-update
  228.3 97.7 %all-gather.2.cloned.1.call-done = f32[64,128,128]{2,1,0:T(8,128)} async-done(((f32[1,128,128]{2,1,0:T(8,128)}), f32[64,128,128]{2,1,0:T(8,128)}) %all-gather.2.cloned.1.call-update) | async-done | bytes 4194320 | tf_op jit(solution)/shard_map/all_gather | solution.py:70
  326.0 0.0 copy-start
  326.0 8.7 %fusion.10 = f32[24,64,128]{2,0,1:T(8,128)S(1)} fusion(f32[64,128,128]{2,1,0:T(8,128)} %all-gather.2.cloned.1.call-done, f32[64]{0:T(128)S(1)} %get-tuple-element.13, f32[128,128]{1,0:T(8,128)S(1)} %fusion.25, f32[64,24,128]{2,1,0:T(8,128)S(1)} %gather_fusion.2), kind=kOutput, calls=%fused_computation.17 | convolution fusion | flops 304087040 | bytes 5832960 | tf_op jit(solution)/shard_map/ckg,kfg->ckf/dot_general | solution.py:31
  334.7 0.6 fusion.20
  335.3 0.0 copy-done
  335.3 4.0 %fusion.9 = f32[24,64,128]{2,0,1:T(8,128)S(1)} fusion(f32[64,128,128]{2,1,0:T(8,128)S(1)} %copy-done, f32[64]{0:T(128)S(1)} %get-tuple-element.13, f32[128,128]{1,0:T(8,128)S(1)} %fusion.25, f32[64,24,128]{2,1,0:T(8,128)S(1)} %gather_fusion.1, f32[64]{0:T(128)S(1)} %get-tuple-element.12), kind=kOutput, calls=%fused_computation.16 | convolution fusion | flops 304283648 | bytes 5833216 | tf_op jit(solution)/shard_map/ckf,kfg->ckg/dot_general | solution.py:34
  339.3 0.6 fusion.13
  339.9 0.1 all_to_all.16
  340.0 1.2 copy.37
  341.2 9.9 %all-to-all-start.1 = ((f32[24,12,512]{2,0,1:T(8,128)}), f32[24,12,512]{2,0,1:T(8,128)}, u32[]{:S(2)}, u32[]{:S(2)}) async-start(f32[24,12,512]{2,0,1:T(8,128)} %copy.37), calls=%async_computation.1 | async-start | bytes 1179648 | tf_op jit(solution)/shard_map/all_to_all | solution.py:73
  351.1 23.3 %all-to-all-done.1 = f32[24,12,512]{2,0,1:T(8,128)} async-done(((f32[24,12,512]{2,0,1:T(8,128)}), f32[24,12,512]{2,0,1:T(8,128)}, u32[]{:S(2)}, u32[]{:S(2)}) %all-to-all-start.1) | async-done | bytes 589856 | tf_op jit(solution)/shard_map/all_to_all | solution.py:73
  374.4 1.9 copy.38
  376.3 7.6 %gather_fusion.3 = f32[2048,24]{1,0:T(8,128)} fusion(f32[24,6144]{0,1:T(8,128)S(1)} %bitcast.50, s32[2048]{0:T(1024)S(1)} %broadcast_clamp_fusion), kind=kCustom, calls=%fused_computation.3 | custom fusion | bytes 401408 | tf_op jit(solution)/shard_map/gather | solution.py:74
  383.9 2.2 copy.39
  (9 shorter events, 0.1 us)
Async XLA Ops:
  15.7 24.3 %copy-start.1 = (s32[1,64,2]{1,2,0:T(2,128)S(1)}, s32[1,64,2]{1,2,0:T(2,128)}, u32[]{:S(2)}) copy-start(s32[1,64,2]{1,2,0:T(2,128)} %param.6) | copy-start | bytes 1540
  15.7 24.4 %copy-start.2 = (s32[1,64]{1,0:T(1,128)S(1)}, s32[1,64]{1,0:T(1,128)}, u32[]{:S(2)}) copy-start(s32[1,64]{1,0:T(1,128)} %param.7) | copy-start | bytes 772
  24.3 38.9 %all-to-all-start = ((f32[24,12,512]{2,0,1:T(8,128)}), f32[24,12,512]{2,0,1:T(8,128)S(1)}, u32[]{:S(2)}, u32[]{:S(2)}) async-start(f32[24,12,512]{2,0,1:T(8,128)} %copy.27), calls=%async_computation | async-start | bytes 1179648 | tf_op jit(solution)/shard_map/all_to_all | solution.py:57
  40.0 186.8 %reduce-scatter.4.cloned.1.call-start = ((), (), s32[]{:S(2)}) async-start(), calls=%async_computation.4 | async-start | bytes 4259840
  73.3 252.7 %all-gather.2.cloned.1.call-start = ((), (), s32[]{:S(2)}) async-start(), calls=%async_computation.3 | async-start | bytes 4259840 | tf_op jit(solution)/shard_map/all_gather | solution.py:70
  326.0 9.3 %copy-start = (f32[64,128,128]{2,1,0:T(8,128)S(1)}, f32[64,128,128]{2,1,0:T(8,128)}, u32[]{:S(2)}) copy-start(f32[64,128,128]{2,1,0:T(8,128)} %all-gather.2.cloned.1.call-done) | copy-start | bytes 12582916
  341.2 33.2 %all-to-all-start.1 = ((f32[24,12,512]{2,0,1:T(8,128)}), f32[24,12,512]{2,0,1:T(8,128)}, u32[]{:S(2)}, u32[]{:S(2)}) async-start(f32[24,12,512]{2,0,1:T(8,128)} %copy.37), calls=%async_computation.1 | async-start | bytes 1179648 | tf_op jit(solution)/shard_map/all_to_all | solution.py:73
Sparse Core Ops, SparseCore 0:
  73.5 153.2 reduce-scatter.3
  231.9 94.0 all-gather.1
where the time goes:
time: 396 us; the launch traced here: 393 us
  waiting for transfers between devices  295 us (74%)
  local copies, waits for them, and re-layouts  27.6 us (7%)
  starting transfers between devices  25.9 us (7%)
  matrix products  22 us (6%)
  between operations  14.2 us (4%)
  other arithmetic  7.7 us (2%)
    unnamed x3, waiting for transfers between devices  153 us
    all_gather x1, waiting for transfers between devices, body(): every_block = lax.all_gather(owned_block, 'group', axis=0, tiled=True)  97.7 us
    all_to_all x1, waiting for transfers between devices, body(): lax.all_to_all(updated, 'region', split_axis=1, concat_axis=1, tiled=True)  23.3 us
    all_to_all x1, waiting for transfers between devices, body(): lax.all_to_all(outgoing, 'region', split_axis=1, concat_axis=1, tiled=True)  21.2 us
    all_to_all x1, starting transfers between devices, body(): lax.all_to_all(outgoing, 'region', split_axis=1, concat_axis=1, tiled=True)  15.7 us
    all_to_all x1, starting transfers between devices, body(): lax.all_to_all(updated, 'region', split_axis=1, concat_axis=1, tiled=True)  9.92 us
    dot_general x1, matrix products, change_of(): jnp.einsum('ckg,kfg->ckf', regional[:, right_idx], shifted, precision=lax...  8.71 us
    dot_general x1, matrix products, margin_of(): jnp.einsum('ckf,ckg->kfg', left_cols, right_cols, precision=lax.Precision...  8.18 us
  transfers between devices with their start and end apart: 4, of which 4 were waited for; matrix products, arithmetic and copies ran while one was open for 0% of the time, Pallas kernels for 0%

commit v1 on v0

v1 whole, which is shorter than its diff:
```python
import functools

import jax
import jax.numpy as jnp
from jax import lax
from jax.experimental import pallas as pl
from jax.experimental.pallas import tpu as pltpu
from jax.sharding import PartitionSpec as P

COEFFICIENT_SIZE = 1536
FB = 128
BPS = 4
FD = 2048
NR = 12
NG = 64
NBLK = NR * BPS
NQ = NG // 4
ROWS = 24
NC = ROWS // 8
NT = 2 * NQ
PACKED = 28
MESH = pl.DeviceIdType.MESH
HIGHEST = lax.Precision.HIGHEST

T_UNIT = 0
T_PERM = T_UNIT + NT
T_SAME = T_PERM + NT
T_LAST = T_SAME + NT
T_IDX = T_LAST + NBLK
T_INV = T_IDX + NT
T_POS = T_INV + NBLK
T_END = T_POS + NG


def slot_index(target):
    onehot = (target[:, None] == jnp.arange(NR, dtype=jnp.int32)[None, :]).astype(jnp.int32)
    rank = jnp.sum((jnp.cumsum(onehot, axis=0) - onehot) * onehot, axis=1)
    return rank, jnp.sum(onehot, axis=0)


def pair_tables(pairs, owners):
    left, right = pairs[:, 0], pairs[:, 1]
    off = left != right
    number = jnp.arange(NG, dtype=jnp.int32)
    off_rank = jnp.sum((off[None, :] & (number[None, :] < number[:, None])).astype(jnp.int32), axis=1)
    pick = (off_rank[None, :] == jnp.arange(NQ, dtype=jnp.int32)[:, None]) & off[None, :]
    unit = jnp.stack(
        [jnp.sum(jnp.where(pick, left[None, :], 0), axis=1), jnp.sum(jnp.where(pick, right[None, :], 0), axis=1)],
        axis=1,
    ).reshape(NT)
    u = jnp.arange(NT, dtype=jnp.int32)
    key = unit * NT + u
    rank = jnp.sum((key[None, :] < key[:, None]).astype(jnp.int32), axis=1)
    at = rank[None, :] == u[:, None]
    perm = jnp.sum(jnp.where(at, u[None, :], 0), axis=1)
    ordered = jnp.sum(jnp.where(at, unit[None, :], 0), axis=1)
    same = jnp.concatenate([jnp.zeros((1,), jnp.int32), (ordered[1:] == ordered[:-1]).astype(jnp.int32)])
    b = jnp.arange(NBLK, dtype=jnp.int32)
    last = jnp.max(jnp.where(ordered[None, :] == b[:, None], u[None, :], -1), axis=1)
    last = jnp.where(last < 0, NT, last)
    piece = jnp.where(off, NBLK + off_rank, left)
    pos = jnp.sum(jnp.where(owners[None, :] == number[:, None], piece[None, :], 0), axis=1)
    return unit, perm, same, last, pos


def kernel(
    tab, x_ref, hi_ref, hip_ref, lo_ref, out_ref, margin_ref,
    oh_lo, masked, zout, zin, gdo, gdi, goo, goi, qd, qo, rdo, rdi, roo, roi, seg, zro, zri,
    mdo, mdi, mzo, mko, mall, mfo, mfi, upd, picked,
    ss, sr_z, sr_gd, sr_go, sr_qd, sr_qo, sr_rd, sr_ro, sr_zr, sr_md, sr_mz, sr_mo, sr_mf,
):
    r = lax.axis_index("region")
    g = lax.axis_index("group")
    me = lax.div(g, 4)
    h = lax.rem(g, 4)

    def z_peer(k):
        return lax.rem(r + k, NR)

    def c_peer(k):
        return lax.rem(me + k, NQ)

    def q_peer(k):
        return lax.rem(h + k, 4)

    barrier = pltpu.get_barrier_semaphore()

    def greet_z(k, _):
        pl.semaphore_signal(barrier, inc=1, device_id=(z_peer(k), g), device_id_type=MESH)
        return 0

    def greet_c(k, _):
        pl.semaphore_signal(barrier, inc=1, device_id=(r, c_peer(k) * 4 + h), device_id_type=MESH)
        return 0

    def greet_q(k, _):
        pl.semaphore_signal(barrier, inc=1, device_id=(r, me * 4 + q_peer(k)), device_id_type=MESH)
        return 0

    lax.fori_loop(1, NR, greet_z, 0)
    lax.fori_loop(1, NQ, greet_c, 0)
    lax.fori_loop(1, 4, greet_q, 0)

    def z_send(src, dst, sem_r, sem_s):
        def go(i, _):
            k = NR // 2 + lax.div(i + 1, 2) * (1 - 2 * lax.rem(i, 2))
            d = z_peer(k)
            pltpu.make_async_remote_copy(
                src_ref=src.at[pl.ds(d * BPS, BPS)], dst_ref=dst.at[pl.ds(r * BPS, BPS)],
                send_sem=sem_s, recv_sem=sem_r, device_id=(d, g), device_id_type=MESH,
            ).start()
            return 0

        lax.fori_loop(0, NR - 1, go, 0)

    def z_wait(src, dst, sem_r, sem_s):
        n = (NR - 1) * BPS
        c = pltpu.make_async_remote_copy(
            src_ref=src.at[pl.ds(0, n)], dst_ref=dst.at[pl.ds(0, n)],
            send_sem=sem_s, recv_sem=sem_r, device_id=(z_peer(1), g), device_id_type=MESH,
        )
        return c

    def c_send(src, dst, sem_r, sem_s, base=0):
        def go(k, _):
            m = c_peer(k)
            pltpu.make_async_remote_copy(
                src_ref=src.at[m], dst_ref=dst.at[base + me],
                send_sem=sem_s, recv_sem=sem_r, device_id=(r, m * 4 + h), device_id_type=MESH,
            ).start()
            return 0

        lax.fori_loop(1, NQ, go, 0)

    def c_wait(src, dst, sem_r, sem_s):
        return pltpu.make_async_remote_copy(
            src_ref=src.at[pl.ds(0, NQ - 1)], dst_ref=dst.at[pl.ds(0, NQ - 1)],
            send_sem=sem_s, recv_sem=sem_r, device_id=(r, c_peer(1) * 4 + h), device_id_type=MESH,
        )

    def q_send(buf, sem_r, sem_s):
        def go(k, _):
            o = q_peer(k)
            pltpu.make_async_remote_copy(
                src_ref=buf.at[h], dst_ref=buf.at[h],
                send_sem=sem_s, recv_sem=sem_r, device_id=(r, me * 4 + o), device_id_type=MESH,
            ).start()
            return 0

        lax.fori_loop(1, 4, go, 0)

    def q_wait(buf, sem_r, sem_s):
        return pltpu.make_async_remote_copy(
            src_ref=buf.at[pl.ds(0, 3)], dst_ref=buf.at[pl.ds(0, 3)],
            send_sem=sem_s, recv_sem=sem_r, device_id=(r, me * 4 + q_peer(1)), device_id_type=MESH,
        )

    zero = jnp.zeros((8, FB), jnp.float32)

    oh_lo[...] = jnp.where(
        lax.broadcasted_iota(jnp.int32, (FB, FD), 0) == lo_ref[...], 1.0, 0.0
    ).astype(jnp.bfloat16)
    hi = hi_ref[...]
    for c in range(NC):
        x = x_ref[pl.ds(8 * c, 8), :]
        big = x.astype(jnp.bfloat16)
        small = (x - big.astype(jnp.float32)).astype(jnp.bfloat16)
        both = jnp.concatenate([big, small], axis=0)
        for b in range(NBLK):
            keep = jnp.where(hi == b, 1.0, 0.0).astype(jnp.bfloat16)
            masked[pl.ds(16 * b, 16), :] = both * keep
        placed = lax.dot_general(
            masked[...], oh_lo[...], (((1,), (1,)), ((), ())), preferred_element_type=jnp.float32
        ).reshape(NBLK, 16, FB)
        zout[c][pl.ds(0, NBLK)] = placed[:, :8] + placed[:, 8:]
        zout[c][NBLK] = zero
        if c == 0:
            pl.semaphore_wait(barrier, (NR - 1) + (NQ - 1) + 3)
        z_send(zout[c], zin[c], sr_z.at[c], ss.at[12 + c])
        zin[c][pl.ds(r * BPS, BPS)] = zout[c][pl.ds(r * BPS, BPS)]

    for t in range(NT):
        for c in range(NC):
            gdo[t // 2, t % 2, c] = zout[c][tab[T_IDX + t]]
    c_send(gdo, gdi, sr_gd, ss.at[1])
    gdi[me] = gdo[me]
    c_wait(gdo, gdi, sr_gd, ss.at[1]).wait_recv()

    def block_of(ref, u):
        return ref[:, u].reshape(NQ * NC * 8, FB)

    def gram(a, b):
        return lax.dot_general(a, b, (((0,), (0,)), ((), ())), precision=HIGHEST, preferred_element_type=jnp.float32)

    for u in range(2):
        xu = block_of(gdi, u)
        qd[h, u] = gram(xu, xu)
    q_send(qd, sr_qd, ss.at[2])

    for c in range(NC):
        z_wait(zout[c], zin[c], sr_z.at[c], ss.at[12 + c]).wait_recv()
        for k in range(NQ):
            for u in range(2):
                goo[c][k, u] = zin[c][tab[T_UNIT + 2 * k + u]]
        c_send(goo[c], goi[c], sr_go.at[c], ss.at[15 + c])
        goi[c][me] = goo[c][me]

    q_wait(qd, sr_qd, ss.at[2]).wait_recv()
    eye = jnp.where(
        lax.broadcasted_iota(jnp.int32, (FB, FB), 0) == lax.broadcasted_iota(jnp.int32, (FB, FB), 1), 1.0, 0.0
    )
    for u in range(2):
        m = (qd[0, u] + qd[1, u] + qd[2, u] + qd[3, u]) * (1.0 / COEFFICIENT_SIZE)
        mdo[:, u] = m.reshape(NQ, 8, FB)
        change = jnp.dot(block_of(gdi, u), m - eye, precision=HIGHEST, preferred_element_type=jnp.float32)
        rdo[:, u] = change.reshape(NQ, NC, 8, FB)
    c_send(mdo, mdi, sr_md, ss.at[4])
    mdi[me] = mdo[me]

    for c in range(NC):
        c_wait(goo[c], goi[c], sr_go.at[c], ss.at[15 + c]).wait_recv()
    left = jnp.concatenate([goi[c][:, 0].reshape(NQ * 8, FB) for c in range(NC)], axis=0)
    right = jnp.concatenate([goi[c][:, 1].reshape(NQ * 8, FB) for c in range(NC)], axis=0)
    qo[h] = gram(left, right)
    q_send(qo, sr_qo, ss.at[5])

    c_wait(mdo, mdi, sr_md, ss.at[4]).wait_recv()
    for b in range(NBLK):
        t = tab[T_INV + b]
        mzo[b] = mdi[lax.div(t, 2), lax.rem(t, 2)]
    z_send(mzo, mall, sr_mz, ss.at[6])
    mall[pl.ds(r * BPS, BPS)] = mzo[pl.ds(r * BPS, BPS)]

    q_wait(qo, sr_qo, ss.at[5]).wait_recv()
    m = (qo[0] + qo[1] + qo[2] + qo[3]) * (1.0 / COEFFICIENT_SIZE)
    mko[...] = m.reshape(NQ, 8, FB)
    to_left = lax.dot_general(
        right, m, (((1,), (1,)), ((), ())), precision=HIGHEST, preferred_element_type=jnp.float32
    ).reshape(NC, NQ, 8, FB)
    to_right = jnp.dot(left, m, precision=HIGHEST, preferred_element_type=jnp.float32).reshape(NC, NQ, 8, FB)
    for c in range(NC):
        roo[c][:, 0] = to_left[c]
        roo[c][:, 1] = to_right[c]
        c_send(roo[c], roi[c], sr_ro.at[c], ss.at[18 + c])
        roi[c][me] = roo[c][me]

    c_send(mko, mall, sr_mo, ss.at[8], base=NBLK)
    mall[NBLK + me] = mko[me]
    c_send(rdo, rdi, sr_rd, ss.at[9])
    rdi[me] = rdo[me]

    seg[NT] = zero
    for c in range(NC):
        c_wait(roo[c], roi[c], sr_ro.at[c], ss.at[18 + c]).wait_recv()
        total = zero
        for i in range(NT):
            p = tab[T_PERM + i]
            total = roi[c][lax.div(p, 2), lax.rem(p, 2)] + total * tab[T_SAME + i].astype(jnp.float32)
            seg[i] = total
        for b in range(NBLK):
            zro[c][b] = seg[tab[T_LAST + b]]
        z_send(zro[c], zri[c], sr_zr.at[c], ss.at[21 + c])
        zri[c][pl.ds(r * BPS, BPS)] = zro[c][pl.ds(r * BPS, BPS)]
        zri[c][NBLK] = zero

    z_wait(mzo, mall, sr_mz, ss.at[6]).wait_recv()
    c_wait(mko, mall, sr_mo, ss.at[8]).wait_recv()
    for i in range(NQ):
        mfo[i] = mall[tab[T_POS + 4 * i + h]]
    c_send(mfo, mfi, sr_mf, ss.at[11])
    mfi[me] = mfo[me]

    c_wait(rdo, rdi, sr_rd, ss.at[9]).wait_recv()
    hip = hip_ref[...]
    for c in range(NC):
        z_wait(zro[c], zri[c], sr_zr.at[c], ss.at[21 + c]).wait_recv()
        for t in range(PACKED):
            u = gdo[t // 2, t % 2, c] - 0.5 * (rdi[t // 2, t % 2, c] + zri[c][tab[T_IDX + t]])
            big = u.astype(jnp.bfloat16)
            small = (u - big.astype(jnp.float32)).astype(jnp.bfloat16)
            upd[pl.ds(16 * t, 16), :] = jnp.concatenate([big, small], axis=0)
        picked[...] = jnp.dot(upd[...], oh_lo[...], preferred_element_type=jnp.float32)
        total = jnp.zeros((8, FD), jnp.float32)
        for t in range(PACKED):
            both = picked[pl.ds(16 * t, 8), :] + picked[pl.ds(16 * t + 8, 8), :]
            total = total + jnp.where(hip == t, both, 0.0)
        out_ref[pl.ds(8 * c, 8), :] = total

    c_wait(mfo, mfi, sr_mf, ss.at[11]).wait_recv()
    margin_ref[...] = mfi[...].reshape(FB, FB)

    for c in range(NC):
        z_wait(zout[c], zin[c], sr_z.at[c], ss.at[12 + c]).wait_send()
        c_wait(goo[c], goi[c], sr_go.at[c], ss.at[15 + c]).wait_send()
        c_wait(roo[c], roi[c], sr_ro.at[c], ss.at[18 + c]).wait_send()
        z_wait(zro[c], zri[c], sr_zr.at[c], ss.at[21 + c]).wait_send()
    c_wait(gdo, gdi, sr_gd, ss.at[1]).wait_send()
    q_wait(qd, sr_qd, ss.at[2]).wait_send()
    c_wait(mdo, mdi, sr_md, ss.at[4]).wait_send()
    q_wait(qo, sr_qo, ss.at[5]).wait_send()
    z_wait(mzo, mall, sr_mz, ss.at[6]).wait_send()
    c_wait(mko, mall, sr_mo, ss.at[8]).wait_send()
    c_wait(rdo, rdi, sr_rd, ss.at[9]).wait_send()
    c_wait(mfo, mfi, sr_mf, ss.at[11]).wait_send()


def body(coeffs, region_of, block_pairs, block_owner):
    target = region_of[:, 0]
    rank, count = slot_index(target)
    blocks = (count + FB - 1) // FB
    d = jnp.arange(NR, dtype=jnp.int32)
    start = jnp.sum(jnp.where(d[None, :] < d[:, None], blocks[None, :], 0), axis=1)
    b = jnp.arange(NBLK, dtype=jnp.int32)
    inv = jnp.where((b % BPS)[None, :].reshape(NR, BPS) < blocks[:, None], start[:, None] + (b % BPS).reshape(NR, BPS), NT - 1)
    inv = inv.reshape(NBLK)
    t = jnp.arange(NT, dtype=jnp.int32)
    idx = jnp.min(jnp.where((inv[None, :] == t[:, None]) & (t[:, None] < NT - 1), b[None, :], NBLK), axis=1)
    unit, perm, same, last, pos = pair_tables(block_pairs[0], block_owner[0])
    tab = jnp.concatenate([unit, perm, same, last, idx, inv, pos]).astype(jnp.int32)
    hi = target * BPS + rank // FB
    hip = jnp.sum(jnp.where(target[:, None] == d[None, :], start[None, :], 0), axis=1) + rank // FB
    lo = rank % FB

    f32, bf16 = jnp.float32, jnp.bfloat16
    v = pltpu.VMEM
    tile = (8, FB)
    dma = pltpu.SemaphoreType.DMA
    vm = pl.BlockSpec(memory_space=pltpu.VMEM)
    z = [v((NBLK + 1, *tile), f32) for _ in range(NC)]
    pr = [v((NQ, 2, *tile), f32) for _ in range(NC)]
    un = v((NQ, 2, NC, *tile), f32)
    corrected, margin = pl.pallas_call(
        kernel,
        out_shape=(jax.ShapeDtypeStruct((ROWS, FD), f32), jax.ShapeDtypeStruct((FB, FB), f32)),
        in_specs=[pl.BlockSpec(memory_space=pltpu.SMEM), vm, vm, vm, vm],
        out_specs=(vm, vm),
        scratch_shapes=[
            v((FB, FD), bf16), v((NBLK * 16, FD), bf16), z, z, un, un, pr, pr,
            v((4, 2, FB, FB), f32), v((4, FB, FB), f32), un, un, pr, pr, v((NT + 1, *tile), f32), z, z,
            v((NQ, 2, *tile), f32), v((NQ, 2, *tile), f32), v((NBLK, *tile), f32), v((NQ, *tile), f32),
            v((NG, *tile), f32), v((NQ, *tile), f32), v((NQ, *tile), f32),
            v((PACKED * 16, FB), bf16), v((PACKED * 16, FD), f32),
            dma((24,)), dma((NC,)), dma, dma((NC,)), dma, dma, dma, dma((NC,)), dma((NC,)), dma, dma, dma, dma,
        ],
        compiler_params=pltpu.CompilerParams(collective_id=0, has_side_effects=True, vmem_limit_bytes=56 * 2**20),
    )(tab, coeffs, hi[None, :], hip[None, :], lo[None, :])
    return corrected, margin[None, None]


def solution(mesh):
    placed = (P("group", "region"), P("region", None), P("region", None, None), P("region", None))
    return jax.shard_map(
        body,
        mesh=mesh,
        in_specs=placed,
        out_specs=(P("group", "region"), P("region", "group", None, None)),
        check_vma=False,
    )
```

time: 396 us -> 100 us (0.25)
  waiting for transfers between devices: 295 us -> 0 us
  Pallas kernels: 0 us -> 86.4 us
  starting transfers between devices: 25.9 us -> 0 us
  local copies, waits for them, and re-layouts: 27.6 us -> 5.08 us
  matrix products: 22 us -> 0 us
  between operations: 14.2 us -> 0.76 us
    unnamed x3 -> x0, waiting for transfers between devices: 153 us -> none
    all_gather x1 -> x0, waiting for transfers between devices: 97.7 us -> none  [body(): every_block = lax.all_gather(owned_block, 'group', axis=0, tiled=True)]
    pallas_call x0 -> x1, Pallas kernels: none -> 86.4 us  [body(): pl.pallas_call(kernel, out_shape=(jax.ShapeDtypeStruct((ROWS, FD), f32),...]
    all_to_all x2 -> x0, waiting for transfers between devices: 44.5 us -> none  [the longest x1 23.3 us: body(): lax.all_to_all(updated, 'region', split_axis=1, concat_axis=1, tiled=True)]
    all_to_all x2 -> x0, starting transfers between devices: 25.6 us -> none  [the longest x1 15.7 us: body(): lax.all_to_all(outgoing, 'region', split_axis=1, concat_axis=1, tiled=True)]
    dot_general x5 -> x0, matrix products: 22 us -> none  [the longest x1 8.71 us: change_of(): jnp.einsum('ckg,kfg->ckf', regional[:, right_idx], shifted, precision=lax...]
    gather x4 -> x0, local copies, waits for them, and re-layouts: 9.45 us -> none  [the longest x1 7.58 us: body(): return (handed_result[:, slot_of], owned_block[None])]
    scatter x2 -> x0, local copies, waits for them, and re-layouts: 7.5 us -> none  [the longest x1 6.73 us: body(): jnp.zeros((coef_rows, slot_count), coeffs.dtype).at[:, slot_of].set(coeffs)]
  transfers between devices with their start and end apart: 4 -> 0, of which waited for: 4 -> 0; matrix products, arithmetic and copies ran while one was open for 0% -> 0% of each run, Pallas kernels for 0% -> 0%
where the time goes in v1:
time: 100 us; the launch traced here: 99.9 us
  Pallas kernels  86.4 us (86%)
  other arithmetic  7.69 us (8%)
  local copies, waits for them, and re-layouts  5.08 us (5%)
    pallas_call x1, Pallas kernels, body(): pl.pallas_call(kernel, out_shape=(jax.ShapeDtypeStruct((ROWS, FD), f32),...  86.4 us
    another operation x3, other arithmetic  3.68 us
    unnamed x12, local copies, waits for them, and re-layouts  3.56 us

profile of v1, /device:TPU:1, one launch (start us, length us, event | category | flops | bytes accessed | tf_op | source)
XLA Modules:
  0.0 99.9 jit_solution(9770079804209305445)
XLA Ops:
  0.6 0.0 copy-start
  0.6 0.8 fusion.6
  1.4 0.0 copy-start.2
  1.4 0.1 convert_reduce_fusion.1
  1.5 0.6 copy-done.2
  2.1 0.0 copy-start.3
  2.1 0.6 copy-done.3
  2.7 0.1 select_reduce_fusion.1
  2.8 0.0 copy-done
  2.9 0.1 convert_reduce_fusion
  3.0 0.1 select_reduce_fusion.6
  3.1 0.1 select_reduce_fusion.8
  3.3 0.1 copy.8
  3.4 0.1 reshape.239
  3.5 0.2 convert_reduce_fusion.2
  3.6 0.1 select_reduce_fusion.4
  3.8 0.1 compare_convert_fusion
  3.8 0.1 select_reduce_fusion.3
  3.9 0.1 lt.98
  4.0 0.1 lt.99
  4.1 0.1 add.124
  4.2 0.1 add.125
  4.3 0.2 select_reduce_fusion.2
  4.5 0.7 concatenate.3.tab
  5.1 3.4 %reduce-window.6 = s32[12,16,128]{2,1,0:T(8,128)S(1)} reduce-window(s32[12,16,128]{2,1,0:T(8,128)S(1)} %fusion.2, s32[]{:T(128)} %constant.74.clone.1), window={size=1x1x128 pad=0_0x0_0x127_0}, to_apply=%region_11.12 | reduce-window | flops 3121152 | bytes 196612 | tf_op jit(solution)/shard_map/reduce-window
  8.6 0.4 slice_reduce_fusion
  8.9 0.2 reduce-window.9
  9.1 0.1 broadcast_add_fusion
  9.3 0.1 select_reduce_fusion
  9.4 0.6 and_select_fusion
  10.0 0.6 fusion.7
  10.6 0.6 bitcast_add_fusion.hi_ref
  11.2 86.4 %shard_map.59 = (f32[24,2048]{1,0:T(8,128)}, f32[128,128]{1,0:T(8,128)}) custom-call(s32[288]{0:T(512)} %concatenate.3.tab, f32[24,2048]{1,0:T(8,128)} %x_ref.1, s32[1,2048]{1,0:T(1,128)} %bitcast_add_fusion.hi_ref, s32[1,2048]{1,0:T(1,128)} %get-tuple-element.14.hip_ref, s32[1,2048]{1,0:T(1,128)} %get-tuple-element.12.lo_ref), custom_call_target="tpu_custom_call" | custom-call | tf_op jit(solution)/shard_map/pallas_call | solution.py:332
  97.7 0.0 copy-start.1
  97.7 1.6 %copy.12 = f32[24,2048]{1,0:T(8,128)} copy(f32[24,2048]{1,0:T(8,128)} %get-tuple-element.22) | data formatting | bytes 393216
  99.3 0.0 copy-done.1
  99.3 0.6 copy.13
  (10 shorter events, 0.1 us)
Async XLA Ops:
  0.6 2.2 %copy-start = (s32[2048,1]{0,1:T(1,128)S(1)}, s32[2048,1]{0,1:T(1,128)}, u32[]{:S(2)}) copy-start(s32[2048,1]{0,1:T(1,128)} %param.5) | copy-start | bytes 24580
  1.4 0.7 copy-start.2
  2.1 0.7 copy-start.3
  97.7 1.7 %copy-start.1 = (f32[128,128]{1,0:T(8,128)S(1)}, f32[128,128]{1,0:T(8,128)}, u32[]{:S(2)}) copy-start(f32[128,128]{1,0:T(8,128)} %get-tuple-element.5) | copy-start | bytes 196612

commit v2 on v1

--- a/solution.py
+++ b/solution.py
@@ -22,50 +22,57 @@
 MESH = pl.DeviceIdType.MESH
 HIGHEST = lax.Precision.HIGHEST
 
-T_UNIT = 0
-T_PERM = T_UNIT + NT
-T_SAME = T_PERM + NT
-T_LAST = T_SAME + NT
-T_IDX = T_LAST + NBLK
-T_INV = T_IDX + NT
-T_POS = T_INV + NBLK
-T_END = T_POS + NG
-
-
-def slot_index(target):
-    onehot = (target[:, None] == jnp.arange(NR, dtype=jnp.int32)[None, :]).astype(jnp.int32)
-    rank = jnp.sum((jnp.cumsum(onehot, axis=0) - onehot) * onehot, axis=1)
-    return rank, jnp.sum(onehot, axis=0)
-
-
-def pair_tables(pairs, owners):
-    left, right = pairs[:, 0], pairs[:, 1]
-    off = left != right
-    number = jnp.arange(NG, dtype=jnp.int32)
-    off_rank = jnp.sum((off[None, :] & (number[None, :] < number[:, None])).astype(jnp.int32), axis=1)
-    pick = (off_rank[None, :] == jnp.arange(NQ, dtype=jnp.int32)[:, None]) & off[None, :]
-    unit = jnp.stack(
-        [jnp.sum(jnp.where(pick, left[None, :], 0), axis=1), jnp.sum(jnp.where(pick, right[None, :], 0), axis=1)],
-        axis=1,
-    ).reshape(NT)
-    u = jnp.arange(NT, dtype=jnp.int32)
-    key = unit * NT + u
-    rank = jnp.sum((key[None, :] < key[:, None]).astype(jnp.int32), axis=1)
-    at = rank[None, :] == u[:, None]
-    perm = jnp.sum(jnp.where(at, u[None, :], 0), axis=1)
-    ordered = jnp.sum(jnp.where(at, unit[None, :], 0), axis=1)
-    same = jnp.concatenate([jnp.zeros((1,), jnp.int32), (ordered[1:] == ordered[:-1]).astype(jnp.int32)])
-    b = jnp.arange(NBLK, dtype=jnp.int32)
-    last = jnp.max(jnp.where(ordered[None, :] == b[:, None], u[None, :], -1), axis=1)
+T_UNIT, T_PERM, T_SAME, T_LAST, T_POS, T_IDX, T_INV = range(7)
+
+
+def iota(shape, axis):
+    return lax.broadcasted_iota(jnp.int32, shape, axis)
+
+
+def column(row, n):
+    spread = jnp.where(iota((n, FB), 0) == iota((n, FB), 1), row, 0)
+    return jnp.sum(spread.astype(jnp.float32), axis=1, keepdims=True).astype(jnp.int32)
+
+
+def pair_rows(left, right, owner_row):
+    p, lane = iota((NG, FB), 0), iota((NG, FB), 1)
+    off = (left != right).astype(jnp.int32)
+    off_row = jnp.sum(jnp.where(p == lane, off, 0), axis=0, keepdims=True)
+    before = jnp.where(lane < p, off_row, 0)
+    off_rank = jnp.sum(before.astype(jnp.float32), axis=1, keepdims=True).astype(jnp.int32)
+    hit = (lane < NT) & (off == 1) & (off_rank == lane % NQ)
+    unit = jnp.sum(jnp.where(hit, jnp.where(lane < NQ, left, right), 0), axis=0, keepdims=True)
+    u, r = iota((NT, FB), 0), iota((NT, FB), 1)
+    dest = column(unit, NT)
+    key_row = unit * NT + iota((1, FB), 1)
+    key = dest * NT + iota((NT, 1), 0)
+    smaller = jnp.where((r < NT) & (key_row < key), 1.0, 0.0)
+    rank = jnp.sum(smaller, axis=1, keepdims=True).astype(jnp.int32)
+    perm = jnp.sum(jnp.where(rank == r, u, 0), axis=0, keepdims=True)
+    here = jnp.sum(jnp.where(rank == r, dest, 0), axis=0, keepdims=True)
+    previous = jnp.sum(jnp.where(rank == r - 1, dest, 0), axis=0, keepdims=True)
+    same = jnp.where((here == previous) & (iota((1, FB), 1) > 0), 1, 0)
+    last = jnp.max(jnp.where(dest == r, rank, -1), axis=0, keepdims=True)
     last = jnp.where(last < 0, NT, last)
-    piece = jnp.where(off, NBLK + off_rank, left)
-    pos = jnp.sum(jnp.where(owners[None, :] == number[:, None], piece[None, :], 0), axis=1)
-    return unit, perm, same, last, pos
+    piece = jnp.where(off == 1, NBLK + off_rank, left)
+    pos = jnp.sum(jnp.where(column(owner_row, NG) == lane, piece, 0), axis=0, keepdims=True)
+    return [unit, perm, same, last, pos]
+
+
+def block_rows(start, blocks):
+    d, t = iota((16, FB), 0), iota((16, FB), 1)
+    inside = (t >= start) & (t < start + blocks)
+    idx = jnp.sum(jnp.where(inside, d * BPS + t - start + 1, 0), axis=0, keepdims=True) - 1
+    idx = jnp.where(idx < 0, NBLK, idx)
+    mine = (t // BPS == d) & (t % BPS < blocks)
+    inv = jnp.sum(jnp.where(mine, start + t % BPS + 1, 0), axis=0, keepdims=True) - 1
+    inv = jnp.where(inv < 0, NT - 1, inv)
+    return [idx, inv]
 
 
 def kernel(
-    tab, x_ref, hi_ref, hip_ref, lo_ref, out_ref, margin_ref,
-    oh_lo, masked, zout, zin, gdo, gdi, goo, goi, qd, qo, rdo, rdi, roo, roi, seg, zro, zri,
+    x_ref, target_ref, pairs_ref, owner_ref, out_ref, margin_ref,
+    tabv, tab, hip_ref, tab_sem, oh_lo, masked, zout, zin, gdo, gdi, goo, goi, qd, qo, rdo, rdi, roo, roi, seg, zro, zri,
     mdo, mdi, mzo, mko, mall, mfo, mfi, upd, picked,
     ss, sr_z, sr_gd, sr_go, sr_qd, sr_qo, sr_rd, sr_ro, sr_zr, sr_md, sr_mz, sr_mo, sr_mf,
 ):
@@ -157,10 +164,23 @@
 
     zero = jnp.zeros((8, FB), jnp.float32)
 
-    oh_lo[...] = jnp.where(
-        lax.broadcasted_iota(jnp.int32, (FB, FD), 0) == lo_ref[...], 1.0, 0.0
-    ).astype(jnp.bfloat16)
-    hi = hi_ref[...]
+    target = target_ref[...]
+    member = jnp.where(iota((16, FD), 0) == target, 1.0, 0.0)
+    parts = [member[:, i * FB : (i + 1) * FB] for i in range(FD // FB)]
+    stacked = jnp.concatenate(parts, axis=0).astype(jnp.bfloat16)
+    lanes = iota((FB, 2 * FB), 1)
+    summing = jnp.where((iota((FB, 2 * FB), 0) < lanes) | (lanes >= FB), 1.0, 0.0).astype(jnp.bfloat16)
+    sums = jnp.dot(stacked, summing, preferred_element_type=jnp.float32)
+    count = jnp.zeros((16, FB), jnp.float32)
+    ranks = []
+    for i, part in enumerate(parts):
+        prefix = sums[16 * i : 16 * i + 16, :FB] + count
+        ranks.append(jnp.sum(part * prefix, axis=0, keepdims=True))
+        count = count + sums[16 * i : 16 * i + 16, FB:]
+    rank = jnp.concatenate(ranks, axis=1).astype(jnp.int32)
+    hi = target * BPS + rank // FB
+    oh_lo[...] = jnp.where(iota((FB, FD), 0) == rank % FB, 1.0, 0.0).astype(jnp.bfloat16)
+
     for c in range(NC):
         x = x_ref[pl.ds(8 * c, 8), :]
         big = x.astype(jnp.bfloat16)
@@ -178,13 +198,28 @@
             pl.semaphore_wait(barrier, (NR - 1) + (NQ - 1) + 3)
         z_send(zout[c], zin[c], sr_z.at[c], ss.at[12 + c])
         zin[c][pl.ds(r * BPS, BPS)] = zout[c][pl.ds(r * BPS, BPS)]
+        if c == 0:
+            blocks = (count.astype(jnp.int32) + (FB - 1)) // FB
+            below = jnp.where(iota((16, 16), 1) < iota((16, 16), 0), 1.0, 0.0).astype(jnp.bfloat16)
+            start = jnp.dot(
+                below, blocks.astype(jnp.float32).astype(jnp.bfloat16), preferred_element_type=jnp.float32
+            )
+            base = [jnp.sum(part * start, axis=0, keepdims=True) for part in parts]
+            hip_ref[...] = jnp.concatenate(base, axis=1).astype(jnp.int32) + rank // FB
+            rows = pair_rows(pairs_ref[:, 0:1], pairs_ref[:, 1:2], owner_ref[...])
+            rows = rows + block_rows(start.astype(jnp.int32), blocks)
+            bounds = [NBLK - 1, NT - 1, 1, NT, NG - 1, NBLK, NT - 1]
+            rows = [jnp.clip(row, 0, high) for row, high in zip(rows, bounds)]
+            tabv[...] = jnp.concatenate(rows + [jnp.zeros((1, FB), jnp.int32)], axis=0)
+            tab_copy = pltpu.make_async_copy(tabv, tab, tab_sem)
+            tab_copy.start()
+    tab_copy.wait()
 
     for t in range(NT):
         for c in range(NC):
-            gdo[t // 2, t % 2, c] = zout[c][tab[T_IDX + t]]
+            gdo[t // 2, t % 2, c] = zout[c][tab[T_IDX, t]]
     c_send(gdo, gdi, sr_gd, ss.at[1])
     gdi[me] = gdo[me]
-    c_wait(gdo, gdi, sr_gd, ss.at[1]).wait_recv()
 
     def block_of(ref, u):
         return ref[:, u].reshape(NQ * NC * 8, FB)
@@ -192,16 +227,17 @@
     def gram(a, b):
         return lax.dot_general(a, b, (((0,), (0,)), ((), ())), precision=HIGHEST, preferred_element_type=jnp.float32)
 
-    for u in range(2):
-        xu = block_of(gdi, u)
-        qd[h, u] = gram(xu, xu)
-    q_send(qd, sr_qd, ss.at[2])
-
-    for c in range(NC):
+    for c in range(NC):
+        if c == NC - 1:
+            c_wait(gdo, gdi, sr_gd, ss.at[1]).wait_recv()
+            for u in range(2):
+                xu = block_of(gdi, u)
+                qd[h, u] = gram(xu, xu)
+            q_send(qd, sr_qd, ss.at[2])
         z_wait(zout[c], zin[c], sr_z.at[c], ss.at[12 + c]).wait_recv()
         for k in range(NQ):
             for u in range(2):
-                goo[c][k, u] = zin[c][tab[T_UNIT + 2 * k + u]]
+                goo[c][k, u] = zin[c][tab[T_UNIT, u * NQ + k]]
         c_send(goo[c], goi[c], sr_go.at[c], ss.at[15 + c])
         goi[c][me] = goo[c][me]
 
@@ -226,7 +262,7 @@
 
     c_wait(mdo, mdi, sr_md, ss.at[4]).wait_recv()
     for b in range(NBLK):
-        t = tab[T_INV + b]
+        t = tab[T_INV, b]
         mzo[b] = mdi[lax.div(t, 2), lax.rem(t, 2)]
     z_send(mzo, mall, sr_mz, ss.at[6])
     mall[pl.ds(r * BPS, BPS)] = mzo[pl.ds(r * BPS, BPS)]
@@ -254,11 +290,11 @@
         c_wait(roo[c], roi[c], sr_ro.at[c], ss.at[18 + c]).wait_recv()
         total = zero
         for i in range(NT):
-            p = tab[T_PERM + i]
-            total = roi[c][lax.div(p, 2), lax.rem(p, 2)] + total * tab[T_SAME + i].astype(jnp.float32)
+            p = tab[T_PERM, i]
+            total = roi[c][lax.rem(p, NQ), lax.div(p, NQ)] + total * tab[T_SAME, i].astype(jnp.float32)
             seg[i] = total
         for b in range(NBLK):
-            zro[c][b] = seg[tab[T_LAST + b]]
+            zro[c][b] = seg[tab[T_LAST, b]]
         z_send(zro[c], zri[c], sr_zr.at[c], ss.at[21 + c])
         zri[c][pl.ds(r * BPS, BPS)] = zro[c][pl.ds(r * BPS, BPS)]
         zri[c][NBLK] = zero
@@ -266,7 +302,7 @@
     z_wait(mzo, mall, sr_mz, ss.at[6]).wait_recv()
     c_wait(mko, mall, sr_mo, ss.at[8]).wait_recv()
     for i in range(NQ):
-        mfo[i] = mall[tab[T_POS + 4 * i + h]]
+        mfo[i] = mall[tab[T_POS, 4 * i + h]]
     c_send(mfo, mfi, sr_mf, ss.at[11])
     mfi[me] = mfo[me]
 
@@ -275,7 +311,7 @@
     for c in range(NC):
         z_wait(zro[c], zri[c], sr_zr.at[c], ss.at[21 + c]).wait_recv()
         for t in range(PACKED):
-            u = gdo[t // 2, t % 2, c] - 0.5 * (rdi[t // 2, t % 2, c] + zri[c][tab[T_IDX + t]])
+            u = gdo[t // 2, t % 2, c] - 0.5 * (rdi[t // 2, t % 2, c] + zri[c][tab[T_IDX, t]])
             big = u.astype(jnp.bfloat16)
             small = (u - big.astype(jnp.float32)).astype(jnp.bfloat16)
             upd[pl.ds(16 * t, 16), :] = jnp.concatenate([big, small], axis=0)
@@ -305,22 +341,7 @@
 
 
 def body(coeffs, region_of, block_pairs, block_owner):
-    target = region_of[:, 0]
-    rank, count = slot_index(target)
-    blocks = (count + FB - 1) // FB
-    d = jnp.arange(NR, dtype=jnp.int32)
-    start = jnp.sum(jnp.where(d[None, :] < d[:, None], blocks[None, :], 0), axis=1)
-    b = jnp.arange(NBLK, dtype=jnp.int32)
-    inv = jnp.where((b % BPS)[None, :].reshape(NR, BPS) < blocks[:, None], start[:, None] + (b % BPS).reshape(NR, BPS), NT - 1)
-    inv = inv.reshape(NBLK)
-    t = jnp.arange(NT, dtype=jnp.int32)
-    idx = jnp.min(jnp.where((inv[None, :] == t[:, None]) & (t[:, None] < NT - 1), b[None, :], NBLK), axis=1)
-    unit, perm, same, last, pos = pair_tables(block_pairs[0], block_owner[0])
-    tab = jnp.concatenate([unit, perm, same, last, idx, inv, pos]).astype(jnp.int32)
-    hi = target * BPS + rank // FB
-    hip = jnp.sum(jnp.where(target[:, None] == d[None, :], start[None, :], 0), axis=1) + rank // FB
-    lo = rank % FB
-
+    owners = jnp.pad(block_owner, ((0, 0), (0, FB - NG)))
     f32, bf16 = jnp.float32, jnp.bfloat16
     v = pltpu.VMEM
     tile = (8, FB)
@@ -332,9 +353,10 @@
     corrected, margin = pl.pallas_call(
         kernel,
         out_shape=(jax.ShapeDtypeStruct((ROWS, FD), f32), jax.ShapeDtypeStruct((FB, FB), f32)),
-        in_specs=[pl.BlockSpec(memory_space=pltpu.SMEM), vm, vm, vm, vm],
+        in_specs=[vm, vm, vm, vm],
         out_specs=(vm, vm),
         scratch_shapes=[
+            v((8, FB), jnp.int32), pltpu.SMEM((8, FB), jnp.int32), v((1, FD), jnp.int32), dma,
             v((FB, FD), bf16), v((NBLK * 16, FD), bf16), z, z, un, un, pr, pr,
             v((4, 2, FB, FB), f32), v((4, FB, FB), f32), un, un, pr, pr, v((NT + 1, *tile), f32), z, z,
             v((NQ, 2, *tile), f32), v((NQ, 2, *tile), f32), v((NBLK, *tile), f32), v((NQ, *tile), f32),
@@ -343,7 +365,7 @@
             dma((24,)), dma((NC,)), dma, dma((NC,)), dma, dma, dma, dma((NC,)), dma((NC,)), dma, dma, dma, dma,
         ],
         compiler_params=pltpu.CompilerParams(collective_id=0, has_side_effects=True, vmem_limit_bytes=56 * 2**20),
-    )(tab, coeffs, hi[None, :], hip[None, :], lo[None, :])
+    )(coeffs, region_of.reshape(1, FD), block_pairs[0], owners)
     return corrected, margin[None, None]
 
 

time: 100 us -> 90.9 us (0.909)
  other arithmetic: 7.69 us -> 0 us
    another operation x4 -> x0, other arithmetic: 3.69 us -> none
    add x3 -> x0, other arithmetic: 1.24 us -> none  [the longest x1 0.63 us: body(): jnp.sum(jnp.where(target[:, None] == d[None, :], start[None, :], 0), axis=1)]
    unnamed x12 -> x8, local copies, waits for them, and re-layouts: 3.56 us -> 3.1 us
where the time goes in v2:
time: 90.9 us; the launch traced here: 90.7 us
  Pallas kernels  85.7 us (94%)
  local copies, waits for them, and re-layouts  4.32 us (5%)
    pallas_call x1, Pallas kernels, body(): pl.pallas_call(kernel, out_shape=(jax.ShapeDtypeStruct((ROWS, FD), f32),...  85.7 us
    unnamed x8, local copies, waits for them, and re-layouts  3.1 us

profile of v2, /device:TPU:1, one launch (start us, length us, event | category | flops | bytes accessed | tf_op | source)
XLA Modules:
  0.0 90.7 jit_solution(8434296693640998505)
XLA Ops:
  0.6 0.0 copy-start.2
  0.6 0.6 copy-done.2
  1.3 0.0 copy-start.1
  1.3 0.5 pad.4.owner_ref
  1.8 0.2 copy-done.1
  2.0 0.7 copy.6.pairs_ref
  2.7 85.7 %shard_map.59 = (f32[24,2048]{1,0:T(8,128)}, f32[128,128]{1,0:T(8,128)}) custom-call(f32[24,2048]{1,0:T(8,128)} %x_ref.1, s32[1,2048]{1,0:T(1,128)} %bitcast.4, s32[64,2]{1,0:T(8,128)} %copy.6.pairs_ref, s32[1,128]{1,0:T(1,128)} %pad.4.owner_ref), custom_call_target="tpu_custom_call" | custom-call | tf_op jit(solution)/shard_map/pallas_call | solution.py:353
  88.4 0.0 copy-start
  88.4 1.6 %copy.9 = f32[24,2048]{1,0:T(8,128)} copy(f32[24,2048]{1,0:T(8,128)} %get-tuple-element.8) | data formatting | bytes 393216
  90.1 0.0 copy-done
  90.1 0.6 copy.10
Async XLA Ops:
  0.6 0.7 copy-start.2
  1.3 0.7 copy-start.1
  88.4 1.7 %copy-start = (f32[128,128]{1,0:T(8,128)S(1)}, f32[128,128]{1,0:T(8,128)}, u32[]{:S(2)}) copy-start(f32[128,128]{1,0:T(8,128)} %get-tuple-element.5) | copy-start | bytes 196612

commit v3 on v2

--- a/solution.py
+++ b/solution.py
@@ -19,6 +19,7 @@
 NC = ROWS // 8
 NT = 2 * NQ
 PACKED = 28
+ND = PACKED // 2
 MESH = pl.DeviceIdType.MESH
 HIGHEST = lax.Precision.HIGHEST
 
@@ -30,15 +31,17 @@
 
 
 def column(row, n):
-    spread = jnp.where(iota((n, FB), 0) == iota((n, FB), 1), row, 0)
+    shape = (n, row.shape[1])
+    spread = jnp.where(iota(shape, 0) == iota(shape, 1), row, 0)
     return jnp.sum(spread.astype(jnp.float32), axis=1, keepdims=True).astype(jnp.int32)
 
 
-def pair_rows(left, right, owner_row):
-    p, lane = iota((NG, FB), 0), iota((NG, FB), 1)
+def pair_rows(left_row, right_row, owner_row):
+    left, right = column(left_row, NG), column(right_row, NG)
+    lane = iota((NG, FB), 1)
     off = (left != right).astype(jnp.int32)
-    off_row = jnp.sum(jnp.where(p == lane, off, 0), axis=0, keepdims=True)
-    before = jnp.where(lane < p, off_row, 0)
+    off_row = (left_row != right_row).astype(jnp.int32)
+    before = jnp.where(iota((NG, NG), 1) < iota((NG, NG), 0), off_row, 0)
     off_rank = jnp.sum(before.astype(jnp.float32), axis=1, keepdims=True).astype(jnp.int32)
     hit = (lane < NT) & (off == 1) & (off_rank == lane % NQ)
     unit = jnp.sum(jnp.where(hit, jnp.where(lane < NQ, left, right), 0), axis=0, keepdims=True)
@@ -73,8 +76,8 @@
 def kernel(
     x_ref, target_ref, pairs_ref, owner_ref, out_ref, margin_ref,
     tabv, tab, hip_ref, tab_sem, oh_lo, masked, zout, zin, gdo, gdi, goo, goi, qd, qo, rdo, rdi, roo, roi, seg, zro, zri,
-    mdo, mdi, mzo, mko, mall, mfo, mfi, upd, picked,
-    ss, sr_z, sr_gd, sr_go, sr_qd, sr_qo, sr_rd, sr_ro, sr_zr, sr_md, sr_mz, sr_mo, sr_mf,
+    mdo, mdi, mzo, mq, mko, moi, mall, mfo, mfi, upd, picked,
+    ss, sr_z, sr_gd, sr_go, sr_qd, sr_qo, sr_rd, sr_ro, sr_zr, sr_md, sr_mz, sr_mq, sr_mo, sr_mf,
 ):
     r = lax.axis_index("region")
     g = lax.axis_index("group")
@@ -108,40 +111,58 @@
     lax.fori_loop(1, NQ, greet_c, 0)
     lax.fori_loop(1, 4, greet_q, 0)
 
-    def z_send(src, dst, sem_r, sem_s):
+    def z_send(src, dst, sem_r, sem_s, n=BPS):
         def go(i, _):
             k = NR // 2 + lax.div(i + 1, 2) * (1 - 2 * lax.rem(i, 2))
             d = z_peer(k)
             pltpu.make_async_remote_copy(
-                src_ref=src.at[pl.ds(d * BPS, BPS)], dst_ref=dst.at[pl.ds(r * BPS, BPS)],
+                src_ref=src.at[pl.ds(d * n, n)], dst_ref=dst.at[pl.ds(r * n, n)],
                 send_sem=sem_s, recv_sem=sem_r, device_id=(d, g), device_id_type=MESH,
             ).start()
             return 0
 
         lax.fori_loop(0, NR - 1, go, 0)
 
-    def z_wait(src, dst, sem_r, sem_s):
-        n = (NR - 1) * BPS
+    def z_wait(src, dst, sem_r, sem_s, n=BPS):
+        n = (NR - 1) * n
         c = pltpu.make_async_remote_copy(
             src_ref=src.at[pl.ds(0, n)], dst_ref=dst.at[pl.ds(0, n)],
             send_sem=sem_s, recv_sem=sem_r, device_id=(z_peer(1), g), device_id_type=MESH,
         )
         return c
 
-    def c_send(src, dst, sem_r, sem_s, base=0):
+    handler = me < ND
+
+    def other_handlers(act):
+        @pl.when(handler)
+        def _():
+            act(ND - 1)
+
+        @pl.when(jnp.logical_not(handler))
+        def _():
+            act(ND)
+
+    def c_send(src, dst, sem_r, sem_s, only=NQ):
         def go(k, _):
             m = c_peer(k)
-            pltpu.make_async_remote_copy(
-                src_ref=src.at[m], dst_ref=dst.at[base + me],
-                send_sem=sem_s, recv_sem=sem_r, device_id=(r, m * 4 + h), device_id_type=MESH,
-            ).start()
+
+            def start():
+                pltpu.make_async_remote_copy(
+                    src_ref=src.at[m], dst_ref=dst.at[me],
+                    send_sem=sem_s, recv_sem=sem_r, device_id=(r, m * 4 + h), device_id_type=MESH,
+                ).start()
+
+            if only < NQ:
+                pl.when(m < only)(start)
+            else:
+                start()
             return 0
 
         lax.fori_loop(1, NQ, go, 0)
 
-    def c_wait(src, dst, sem_r, sem_s):
+    def c_wait(src, dst, sem_r, sem_s, n=NQ - 1):
         return pltpu.make_async_remote_copy(
-            src_ref=src.at[pl.ds(0, NQ - 1)], dst_ref=dst.at[pl.ds(0, NQ - 1)],
+            src_ref=src.at[pl.ds(0, n)], dst_ref=dst.at[pl.ds(0, n)],
             send_sem=sem_s, recv_sem=sem_r, device_id=(r, c_peer(1) * 4 + h), device_id_type=MESH,
         )
 
@@ -206,7 +227,7 @@
             )
             base = [jnp.sum(part * start, axis=0, keepdims=True) for part in parts]
             hip_ref[...] = jnp.concatenate(base, axis=1).astype(jnp.int32) + rank // FB
-            rows = pair_rows(pairs_ref[:, 0:1], pairs_ref[:, 1:2], owner_ref[...])
+            rows = pair_rows(pairs_ref[0:1, :], pairs_ref[1:2, :], owner_ref[...])
             rows = rows + block_rows(start.astype(jnp.int32), blocks)
             bounds = [NBLK - 1, NT - 1, 1, NT, NG - 1, NBLK, NT - 1]
             rows = [jnp.clip(row, 0, high) for row, high in zip(rows, bounds)]
@@ -215,11 +236,11 @@
             tab_copy.start()
     tab_copy.wait()
 
-    for t in range(NT):
+    for t in range(PACKED):
         for c in range(NC):
             gdo[t // 2, t % 2, c] = zout[c][tab[T_IDX, t]]
-    c_send(gdo, gdi, sr_gd, ss.at[1])
-    gdi[me] = gdo[me]
+    c_send(gdo, gdi, sr_gd, ss.at[1], only=ND)
+    mdi[NQ - 1, 1] = zero
 
     def block_of(ref, u):
         return ref[:, u].reshape(NQ * NC * 8, FB)
@@ -229,11 +250,17 @@
 
     for c in range(NC):
         if c == NC - 1:
-            c_wait(gdo, gdi, sr_gd, ss.at[1]).wait_recv()
-            for u in range(2):
-                xu = block_of(gdi, u)
-                qd[h, u] = gram(xu, xu)
-            q_send(qd, sr_qd, ss.at[2])
+
+
+            @pl.when(handler)
+            def _():
+                gdi[me] = gdo[me]
+                c_wait(gdo, gdi, sr_gd, ss.at[1]).wait_recv()
+                for u in range(2):
+                    xu = block_of(gdi, u)
+                    qd[h, u] = gram(xu, xu)
+                q_send(qd, sr_qd, ss.at[2])
+
         z_wait(zout[c], zin[c], sr_z.at[c], ss.at[12 + c]).wait_recv()
         for k in range(NQ):
             for u in range(2):
@@ -241,17 +268,17 @@
         c_send(goo[c], goi[c], sr_go.at[c], ss.at[15 + c])
         goi[c][me] = goo[c][me]
 
-    q_wait(qd, sr_qd, ss.at[2]).wait_recv()
-    eye = jnp.where(
-        lax.broadcasted_iota(jnp.int32, (FB, FB), 0) == lax.broadcasted_iota(jnp.int32, (FB, FB), 1), 1.0, 0.0
-    )
-    for u in range(2):
-        m = (qd[0, u] + qd[1, u] + qd[2, u] + qd[3, u]) * (1.0 / COEFFICIENT_SIZE)
-        mdo[:, u] = m.reshape(NQ, 8, FB)
-        change = jnp.dot(block_of(gdi, u), m - eye, precision=HIGHEST, preferred_element_type=jnp.float32)
-        rdo[:, u] = change.reshape(NQ, NC, 8, FB)
-    c_send(mdo, mdi, sr_md, ss.at[4])
-    mdi[me] = mdo[me]
+    @pl.when(handler)
+    def _():
+        q_wait(qd, sr_qd, ss.at[2]).wait_recv()
+        eye = jnp.where(iota((FB, FB), 0) == iota((FB, FB), 1), 1.0, 0.0)
+        for u in range(2):
+            m = (qd[0, u] + qd[1, u] + qd[2, u] + qd[3, u]) * (1.0 / COEFFICIENT_SIZE)
+            mdo[:, u] = m.reshape(NQ, 8, FB)
+            change = jnp.dot(block_of(gdi, u), m - eye, precision=HIGHEST, preferred_element_type=jnp.float32)
+            rdo[:, u] = change.reshape(NQ, NC, 8, FB)
+        c_send(mdo, mdi, sr_md, ss.at[4])
+        mdi[me] = mdo[me]
 
     for c in range(NC):
         c_wait(goo[c], goi[c], sr_go.at[c], ss.at[15 + c]).wait_recv()
@@ -260,12 +287,12 @@
     qo[h] = gram(left, right)
     q_send(qo, sr_qo, ss.at[5])
 
-    c_wait(mdo, mdi, sr_md, ss.at[4]).wait_recv()
-    for b in range(NBLK):
-        t = tab[T_INV, b]
-        mzo[b] = mdi[lax.div(t, 2), lax.rem(t, 2)]
-    z_send(mzo, mall, sr_mz, ss.at[6])
-    mall[pl.ds(r * BPS, BPS)] = mzo[pl.ds(r * BPS, BPS)]
+    other_handlers(lambda n: c_wait(mdo, mdi, sr_md, ss.at[4], n).wait_recv())
+    for d in range(NR):
+        t = tab[T_INV, d * BPS + h]
+        mzo[d] = mdi[lax.div(t, 2), lax.rem(t, 2)]
+    z_send(mzo, mq.at[h], sr_mz, ss.at[6], 1)
+    mq[h, r] = mzo[r]
 
     q_wait(qo, sr_qo, ss.at[5]).wait_recv()
     m = (qo[0] + qo[1] + qo[2] + qo[3]) * (1.0 / COEFFICIENT_SIZE)
@@ -280,10 +307,13 @@
         c_send(roo[c], roi[c], sr_ro.at[c], ss.at[18 + c])
         roi[c][me] = roo[c][me]
 
-    c_send(mko, mall, sr_mo, ss.at[8], base=NBLK)
-    mall[NBLK + me] = mko[me]
-    c_send(rdo, rdi, sr_rd, ss.at[9])
-    rdi[me] = rdo[me]
+    c_send(mko, moi, sr_mo, ss.at[8])
+    moi[me] = mko[me]
+
+    @pl.when(handler)
+    def _():
+        c_send(rdo, rdi, sr_rd, ss.at[9])
+        rdi[me] = rdo[me]
 
     seg[NT] = zero
     for c in range(NC):
@@ -299,14 +329,19 @@
         zri[c][pl.ds(r * BPS, BPS)] = zro[c][pl.ds(r * BPS, BPS)]
         zri[c][NBLK] = zero
 
-    z_wait(mzo, mall, sr_mz, ss.at[6]).wait_recv()
-    c_wait(mko, mall, sr_mo, ss.at[8]).wait_recv()
+    z_wait(mzo, mq.at[h], sr_mz, ss.at[6], 1).wait_recv()
+    q_send(mq, sr_mq, ss.at[0])
+    c_wait(mko, moi, sr_mo, ss.at[8]).wait_recv()
+    q_wait(mq, sr_mq, ss.at[0]).wait_recv()
+    for b in range(NBLK):
+        mall[b] = mq[b % BPS, b // BPS]
+    mall[pl.ds(NBLK, NQ)] = moi[...]
     for i in range(NQ):
         mfo[i] = mall[tab[T_POS, 4 * i + h]]
     c_send(mfo, mfi, sr_mf, ss.at[11])
     mfi[me] = mfo[me]
 
-    c_wait(rdo, rdi, sr_rd, ss.at[9]).wait_recv()
+    other_handlers(lambda n: c_wait(rdo, rdi, sr_rd, ss.at[9], n).wait_recv())
     hip = hip_ref[...]
     for c in range(NC):
         z_wait(zro[c], zri[c], sr_zr.at[c], ss.at[21 + c]).wait_recv()
@@ -330,18 +365,22 @@
         c_wait(goo[c], goi[c], sr_go.at[c], ss.at[15 + c]).wait_send()
         c_wait(roo[c], roi[c], sr_ro.at[c], ss.at[18 + c]).wait_send()
         z_wait(zro[c], zri[c], sr_zr.at[c], ss.at[21 + c]).wait_send()
-    c_wait(gdo, gdi, sr_gd, ss.at[1]).wait_send()
-    q_wait(qd, sr_qd, ss.at[2]).wait_send()
-    c_wait(mdo, mdi, sr_md, ss.at[4]).wait_send()
+    other_handlers(lambda n: c_wait(gdo, gdi, sr_gd, ss.at[1], n).wait_send())
+
+    @pl.when(handler)
+    def _():
+        q_wait(qd, sr_qd, ss.at[2]).wait_send()
+        c_wait(mdo, mdi, sr_md, ss.at[4]).wait_send()
+        c_wait(rdo, rdi, sr_rd, ss.at[9]).wait_send()
+
     q_wait(qo, sr_qo, ss.at[5]).wait_send()
-    z_wait(mzo, mall, sr_mz, ss.at[6]).wait_send()
-    c_wait(mko, mall, sr_mo, ss.at[8]).wait_send()
-    c_wait(rdo, rdi, sr_rd, ss.at[9]).wait_send()
+    z_wait(mzo, mq.at[h], sr_mz, ss.at[6], 1).wait_send()
+    c_wait(mko, moi, sr_mo, ss.at[8]).wait_send()
+    q_wait(mq, sr_mq, ss.at[0]).wait_send()
     c_wait(mfo, mfi, sr_mf, ss.at[11]).wait_send()
 
 
 def body(coeffs, region_of, block_pairs, block_owner):
-    owners = jnp.pad(block_owner, ((0, 0), (0, FB - NG)))
     f32, bf16 = jnp.float32, jnp.bfloat16
     v = pltpu.VMEM
     tile = (8, FB)
@@ -359,13 +398,13 @@
             v((8, FB), jnp.int32), pltpu.SMEM((8, FB), jnp.int32), v((1, FD), jnp.int32), dma,
             v((FB, FD), bf16), v((NBLK * 16, FD), bf16), z, z, un, un, pr, pr,
             v((4, 2, FB, FB), f32), v((4, FB, FB), f32), un, un, pr, pr, v((NT + 1, *tile), f32), z, z,
-            v((NQ, 2, *tile), f32), v((NQ, 2, *tile), f32), v((NBLK, *tile), f32), v((NQ, *tile), f32),
-            v((NG, *tile), f32), v((NQ, *tile), f32), v((NQ, *tile), f32),
+            v((NQ, 2, *tile), f32), v((NQ, 2, *tile), f32), v((NR, *tile), f32), v((4, NR, *tile), f32),
+            v((NQ, *tile), f32), v((NQ, *tile), f32), v((NG, *tile), f32), v((NQ, *tile), f32), v((NQ, *tile), f32),
             v((PACKED * 16, FB), bf16), v((PACKED * 16, FD), f32),
-            dma((24,)), dma((NC,)), dma, dma((NC,)), dma, dma, dma, dma((NC,)), dma((NC,)), dma, dma, dma, dma,
+            dma((24,)), dma((NC,)), dma, dma((NC,)), dma, dma, dma, dma((NC,)), dma((NC,)), dma, dma, dma, dma, dma,
         ],
         compiler_params=pltpu.CompilerParams(collective_id=0, has_side_effects=True, vmem_limit_bytes=56 * 2**20),
-    )(coeffs, region_of.reshape(1, FD), block_pairs[0], owners)
+    )(coeffs, region_of.reshape(1, FD), block_pairs[0].T, block_owner)
     return corrected, margin[None, None]
 
 

time: 90.9 us -> 88.8 us (0.977)
  local copies, waits for them, and re-layouts: 4.32 us -> 2.28 us
    unnamed x8 -> x4, local copies, waits for them, and re-layouts: 3.1 us -> 2.28 us
where the time goes in v3:
time: 88.8 us; the launch traced here: 88.7 us
  Pallas kernels  85.7 us (97%)
  local copies, waits for them, and re-layouts  2.28 us (3%)
    pallas_call x1, Pallas kernels, body(): pl.pallas_call(kernel, out_shape=(jax.ShapeDtypeStruct((ROWS, FD), f32),...  85.7 us
    unnamed x4, local copies, waits for them, and re-layouts  2.28 us

profile of v3, /device:TPU:1, one launch (start us, length us, event | category | flops | bytes accessed | tf_op | source)
XLA Modules:
  0.0 88.7 jit_solution(17568623196464770483)
XLA Ops:
  0.6 85.7 %shard_map.59 = (f32[24,2048]{1,0:T(8,128)}, f32[128,128]{1,0:T(8,128)}) custom-call(f32[24,2048]{1,0:T(8,128)} %x_ref.1, s32[1,2048]{1,0:T(1,128)} %bitcast.6, s32[2,64]{1,0:T(2,128)} %bitcast.7, s32[1,64]{1,0:T(1,128)} %owner_ref.1), custom_call_target="tpu_custom_call" | custom-call | tf_op jit(solution)/shard_map/pallas_call | solution.py:392
  86.4 0.0 copy-start
  86.4 1.6 %copy.8 = f32[24,2048]{1,0:T(8,128)} copy(f32[24,2048]{1,0:T(8,128)} %get-tuple-element.8) | data formatting | bytes 393216
  88.0 0.0 copy-done
  88.0 0.6 copy.9
Async XLA Ops:
  86.4 1.7 %copy-start = (f32[128,128]{1,0:T(8,128)S(1)}, f32[128,128]{1,0:T(8,128)}, u32[]{:S(2)}) copy-start(f32[128,128]{1,0:T(8,128)} %get-tuple-element.5) | copy-start | bytes 196612

commit v4 on v3

--- a/solution.py
+++ b/solution.py
@@ -74,7 +74,7 @@
 
 
 def kernel(
-    x_ref, target_ref, pairs_ref, owner_ref, out_ref, margin_ref,
+    x_ref, target_ref, pairs_ref, owner_ref, big_ref, small_ref, margin_ref,
     tabv, tab, hip_ref, tab_sem, oh_lo, masked, zout, zin, gdo, gdi, goo, goi, qd, qo, rdo, rdi, roo, roi, seg, zro, zri,
     mdo, mdi, mzo, mq, mko, moi, mall, mfo, mfi, upd, picked,
     ss, sr_z, sr_gd, sr_go, sr_qd, sr_qo, sr_rd, sr_ro, sr_zr, sr_md, sr_mz, sr_mq, sr_mo, sr_mf,
@@ -273,18 +273,20 @@
         q_wait(qd, sr_qd, ss.at[2]).wait_recv()
         eye = jnp.where(iota((FB, FB), 0) == iota((FB, FB), 1), 1.0, 0.0)
         for u in range(2):
-            m = (qd[0, u] + qd[1, u] + qd[2, u] + qd[3, u]) * (1.0 / COEFFICIENT_SIZE)
+            m = qd[0, u] + qd[1, u] + qd[2, u] + qd[3, u]
             mdo[:, u] = m.reshape(NQ, 8, FB)
-            change = jnp.dot(block_of(gdi, u), m - eye, precision=HIGHEST, preferred_element_type=jnp.float32)
+            shift = m * (1.0 / COEFFICIENT_SIZE) - eye
+            change = jnp.dot(block_of(gdi, u), shift, precision=HIGHEST, preferred_element_type=jnp.float32)
             rdo[:, u] = change.reshape(NQ, NC, 8, FB)
         c_send(mdo, mdi, sr_md, ss.at[4])
         mdi[me] = mdo[me]
 
+    total = None
     for c in range(NC):
         c_wait(goo[c], goi[c], sr_go.at[c], ss.at[15 + c]).wait_recv()
-    left = jnp.concatenate([goi[c][:, 0].reshape(NQ * 8, FB) for c in range(NC)], axis=0)
-    right = jnp.concatenate([goi[c][:, 1].reshape(NQ * 8, FB) for c in range(NC)], axis=0)
-    qo[h] = gram(left, right)
+        part = gram(goi[c][:, 0].reshape(NQ * 8, FB), goi[c][:, 1].reshape(NQ * 8, FB))
+        total = part if total is None else total + part
+    qo[h] = total
     q_send(qo, sr_qo, ss.at[5])
 
     other_handlers(lambda n: c_wait(mdo, mdi, sr_md, ss.at[4], n).wait_recv())
@@ -295,15 +297,16 @@
     mq[h, r] = mzo[r]
 
     q_wait(qo, sr_qo, ss.at[5]).wait_recv()
-    m = (qo[0] + qo[1] + qo[2] + qo[3]) * (1.0 / COEFFICIENT_SIZE)
+    m = qo[0] + qo[1] + qo[2] + qo[3]
     mko[...] = m.reshape(NQ, 8, FB)
-    to_left = lax.dot_general(
-        right, m, (((1,), (1,)), ((), ())), precision=HIGHEST, preferred_element_type=jnp.float32
-    ).reshape(NC, NQ, 8, FB)
-    to_right = jnp.dot(left, m, precision=HIGHEST, preferred_element_type=jnp.float32).reshape(NC, NQ, 8, FB)
-    for c in range(NC):
-        roo[c][:, 0] = to_left[c]
-        roo[c][:, 1] = to_right[c]
+    m = m * (1.0 / COEFFICIENT_SIZE)
+    for c in range(NC):
+        lc, rc = goi[c][:, 0].reshape(NQ * 8, FB), goi[c][:, 1].reshape(NQ * 8, FB)
+        to_left = lax.dot_general(
+            rc, m, (((1,), (1,)), ((), ())), precision=HIGHEST, preferred_element_type=jnp.float32
+        )
+        roo[c][:, 0] = to_left.reshape(NQ, 8, FB)
+        roo[c][:, 1] = jnp.dot(lc, m, precision=HIGHEST, preferred_element_type=jnp.float32).reshape(NQ, 8, FB)
         c_send(roo[c], roi[c], sr_ro.at[c], ss.at[18 + c])
         roi[c][me] = roo[c][me]
 
@@ -351,11 +354,11 @@
             small = (u - big.astype(jnp.float32)).astype(jnp.bfloat16)
             upd[pl.ds(16 * t, 16), :] = jnp.concatenate([big, small], axis=0)
         picked[...] = jnp.dot(upd[...], oh_lo[...], preferred_element_type=jnp.float32)
-        total = jnp.zeros((8, FD), jnp.float32)
-        for t in range(PACKED):
-            both = picked[pl.ds(16 * t, 8), :] + picked[pl.ds(16 * t + 8, 8), :]
-            total = total + jnp.where(hip == t, both, 0.0)
-        out_ref[pl.ds(8 * c, 8), :] = total
+        for part, ref in enumerate((big_ref, small_ref)):
+            total = jnp.zeros((8, FD), jnp.float32)
+            for t in range(PACKED):
+                total = total + jnp.where(hip == t, picked[pl.ds(16 * t + 8 * part, 8), :], 0.0)
+            ref[pl.ds(8 * c, 8), :] = total
 
     c_wait(mfo, mfi, sr_mf, ss.at[11]).wait_recv()
     margin_ref[...] = mfi[...].reshape(FB, FB)
@@ -389,11 +392,15 @@
     z = [v((NBLK + 1, *tile), f32) for _ in range(NC)]
     pr = [v((NQ, 2, *tile), f32) for _ in range(NC)]
     un = v((NQ, 2, NC, *tile), f32)
-    corrected, margin = pl.pallas_call(
+    big, small, margin = pl.pallas_call(
         kernel,
-        out_shape=(jax.ShapeDtypeStruct((ROWS, FD), f32), jax.ShapeDtypeStruct((FB, FB), f32)),
+        out_shape=(
+            jax.ShapeDtypeStruct((ROWS, FD), f32),
+            jax.ShapeDtypeStruct((ROWS, FD), f32),
+            jax.ShapeDtypeStruct((FB, FB), f32),
+        ),
         in_specs=[vm, vm, vm, vm],
-        out_specs=(vm, vm),
+        out_specs=(vm, vm, vm),
         scratch_shapes=[
             v((8, FB), jnp.int32), pltpu.SMEM((8, FB), jnp.int32), v((1, FD), jnp.int32), dma,
             v((FB, FD), bf16), v((NBLK * 16, FD), bf16), z, z, un, un, pr, pr,
@@ -405,7 +412,7 @@
         ],
         compiler_params=pltpu.CompilerParams(collective_id=0, has_side_effects=True, vmem_limit_bytes=56 * 2**20),
     )(coeffs, region_of.reshape(1, FD), block_pairs[0].T, block_owner)
-    return corrected, margin[None, None]
+    return big + small, (margin * (1.0 / COEFFICIENT_SIZE))[None, None]
 
 
 def solution(mesh):

time: 88.8 us -> 88.8 us (level)
  other arithmetic: 0 us -> 2.39 us
  local copies, waits for them, and re-layouts: 2.28 us -> 0.01 us
    unnamed x4 -> x2, local copies, waits for them, and re-layouts: 2.28 us -> 0.01 us
    add x0 -> x1, other arithmetic: none -> 1.75 us  [body(): return (big + small, (margin * (1.0 / COEFFICIENT_SIZE))[None, None])]
where the time goes in v4:
time: 88.8 us; the launch traced here: 88.6 us
  Pallas kernels  85.6 us (96%)
  other arithmetic  2.39 us (3%)
    pallas_call x1, Pallas kernels, body(): pl.pallas_call(kernel, out_shape=(jax.ShapeDtypeStruct((ROWS, FD), f32),...  85.6 us

profile of v4, /device:TPU:1, one launch (start us, length us, event | category | flops | bytes accessed | tf_op | source)
XLA Modules:
  0.0 88.6 jit_solution(15435930836344132001)
XLA Ops:
  0.6 85.6 %shard_map.59 = (f32[24,2048]{1,0:T(8,128)}, f32[24,2048]{1,0:T(8,128)}, f32[128,128]{1,0:T(8,128)}) custom-call(f32[24,2048]{1,0:T(8,128)} %x_ref.1, s32[1,2048]{1,0:T(1,128)} %bitcast.6, s32[2,64]{1,0:T(2,128)} %bitcast.7, s32[1,64]{1,0:T(1,128)} %owner_ref.1), custom_call_target="tpu_custom_call" | custom-call | tf_op jit(solution)/shard_map/pallas_call | solution.py:395
  86.2 0.0 copy-start
  86.2 1.8 %add.3 = f32[24,2048]{1,0:T(8,128)} add(f32[24,2048]{1,0:T(8,128)} %get-tuple-element.5, f32[24,2048]{1,0:T(8,128)} %get-tuple-element.6) | non-fusion elementwise | flops 49152 | bytes 589824 | tf_op jit(solution)/shard_map/add | solution.py:415
  88.0 0.0 copy-done
  88.0 0.6 multiply_bitcast_fusion
Async XLA Ops:
  86.2 1.8 %copy-start = (f32[128,128]{1,0:T(8,128)S(1)}, f32[128,128]{1,0:T(8,128)}, u32[]{:S(2)}) copy-start(f32[128,128]{1,0:T(8,128)} %get-tuple-element.7) | copy-start | bytes 196612

commit v5 on v4

--- a/solution.py
+++ b/solution.py
@@ -143,8 +143,8 @@
             act(ND)
 
     def c_send(src, dst, sem_r, sem_s, only=NQ):
-        def go(k, _):
-            m = c_peer(k)
+        def go(i, _):
+            m = c_peer(NQ // 2 + lax.div(i + 1, 2) * (1 - 2 * lax.rem(i, 2)))
 
             def start():
                 pltpu.make_async_remote_copy(
@@ -158,7 +158,7 @@
                 start()
             return 0
 
-        lax.fori_loop(1, NQ, go, 0)
+        lax.fori_loop(0, NQ - 1, go, 0)
 
     def c_wait(src, dst, sem_r, sem_s, n=NQ - 1):
         return pltpu.make_async_remote_copy(

time: 88.8 us -> 87.4 us (0.984)
  Pallas kernels: 85.6 us -> 84.2 us
    pallas_call x1, Pallas kernels: 85.6 us -> 84.2 us  [body(): pl.pallas_call(kernel, out_shape=(jax.ShapeDtypeStruct((ROWS, FD), f32),...]
where the time goes in v5:
time: 87.4 us; the launch traced here: 87.2 us
  Pallas kernels  84.2 us (96%)
  other arithmetic  2.39 us (3%)
    pallas_call x1, Pallas kernels, body(): pl.pallas_call(kernel, out_shape=(jax.ShapeDtypeStruct((ROWS, FD), f32),...  84.2 us
    add x1, other arithmetic, body(): return (big + small, (margin * (1.0 / COEFFICIENT_SIZE))[None, None])  1.75 us

profile of v5, /device:TPU:1, one launch (start us, length us, event | category | flops | bytes accessed | tf_op | source)
XLA Modules:
  0.0 87.2 jit_solution(320639800807782475)
XLA Ops:
  0.6 84.2 %shard_map.59 = (f32[24,2048]{1,0:T(8,128)}, f32[24,2048]{1,0:T(8,128)}, f32[128,128]{1,0:T(8,128)}) custom-call(f32[24,2048]{1,0:T(8,128)} %x_ref.1, s32[1,2048]{1,0:T(1,128)} %bitcast.6, s32[2,64]{1,0:T(2,128)} %bitcast.7, s32[1,64]{1,0:T(1,128)} %owner_ref.1), custom_call_target="tpu_custom_call" | custom-call | tf_op jit(solution)/shard_map/pallas_call | solution.py:395
  84.8 0.0 copy-start
  84.8 1.8 %add.3 = f32[24,2048]{1,0:T(8,128)} add(f32[24,2048]{1,0:T(8,128)} %get-tuple-element.5, f32[24,2048]{1,0:T(8,128)} %get-tuple-element.6) | non-fusion elementwise | flops 49152 | bytes 589824 | tf_op jit(solution)/shard_map/add | solution.py:415
  86.6 0.0 copy-done
  86.6 0.6 multiply_bitcast_fusion
Async XLA Ops:
  84.8 1.8 %copy-start = (f32[128,128]{1,0:T(8,128)S(1)}, f32[128,128]{1,0:T(8,128)}, u32[]{:S(2)}) copy-start(f32[128,128]{1,0:T(8,128)} %get-tuple-element.7) | copy-start | bytes 196612

commit v6 on v5

--- a/solution.py
+++ b/solution.py
@@ -268,6 +268,14 @@
         c_send(goo[c], goi[c], sr_go.at[c], ss.at[15 + c])
         goi[c][me] = goo[c][me]
 
+    total = None
+    for c in range(NC):
+        c_wait(goo[c], goi[c], sr_go.at[c], ss.at[15 + c]).wait_recv()
+        part = gram(goi[c][:, 0].reshape(NQ * 8, FB), goi[c][:, 1].reshape(NQ * 8, FB))
+        total = part if total is None else total + part
+    qo[h] = total
+    q_send(qo, sr_qo, ss.at[5])
+
     @pl.when(handler)
     def _():
         q_wait(qd, sr_qd, ss.at[2]).wait_recv()
@@ -281,20 +289,6 @@
         c_send(mdo, mdi, sr_md, ss.at[4])
         mdi[me] = mdo[me]
 
-    total = None
-    for c in range(NC):
-        c_wait(goo[c], goi[c], sr_go.at[c], ss.at[15 + c]).wait_recv()
-        part = gram(goi[c][:, 0].reshape(NQ * 8, FB), goi[c][:, 1].reshape(NQ * 8, FB))
-        total = part if total is None else total + part
-    qo[h] = total
-    q_send(qo, sr_qo, ss.at[5])
-
-    other_handlers(lambda n: c_wait(mdo, mdi, sr_md, ss.at[4], n).wait_recv())
-    for d in range(NR):
-        t = tab[T_INV, d * BPS + h]
-        mzo[d] = mdi[lax.div(t, 2), lax.rem(t, 2)]
-    z_send(mzo, mq.at[h], sr_mz, ss.at[6], 1)
-    mq[h, r] = mzo[r]
 
     q_wait(qo, sr_qo, ss.at[5]).wait_recv()
     m = qo[0] + qo[1] + qo[2] + qo[3]
@@ -317,6 +311,13 @@
     def _():
         c_send(rdo, rdi, sr_rd, ss.at[9])
         rdi[me] = rdo[me]
+
+    other_handlers(lambda n: c_wait(mdo, mdi, sr_md, ss.at[4], n).wait_recv())
+    for d in range(NR):
+        t = tab[T_INV, d * BPS + h]
+        mzo[d] = mdi[lax.div(t, 2), lax.rem(t, 2)]
+    z_send(mzo, mq.at[h], sr_mz, ss.at[6], 1)
+    mq[h, r] = mzo[r]
 
     seg[NT] = zero
     for c in range(NC):

time: 87.4 us -> 87.6 us (level)
  no operation moved by 1% of the time
where the time goes in v6:
time: 87.6 us; the launch traced here: 87.5 us
  Pallas kernels  84.4 us (96%)
  other arithmetic  2.39 us (3%)
    pallas_call x1, Pallas kernels, body(): pl.pallas_call(kernel, out_shape=(jax.ShapeDtypeStruct((ROWS, FD), f32),...  84.4 us
    add x1, other arithmetic, body(): return (big + small, (margin * (1.0 / COEFFICIENT_SIZE))[None, None])  1.75 us

profile of v6, /device:TPU:1, one launch (start us, length us, event | category | flops | bytes accessed | tf_op | source)
XLA Modules:
  0.0 87.5 jit_solution(12072171131084982)
XLA Ops:
  0.6 84.4 %shard_map.59 = (f32[24,2048]{1,0:T(8,128)}, f32[24,2048]{1,0:T(8,128)}, f32[128,128]{1,0:T(8,128)}) custom-call(f32[24,2048]{1,0:T(8,128)} %x_ref.1, s32[1,2048]{1,0:T(1,128)} %bitcast.6, s32[2,64]{1,0:T(2,128)} %bitcast.7, s32[1,64]{1,0:T(1,128)} %owner_ref.1), custom_call_target="tpu_custom_call" | custom-call | tf_op jit(solution)/shard_map/pallas_call | solution.py:396
  85.1 0.0 copy-start
  85.1 1.8 %add.3 = f32[24,2048]{1,0:T(8,128)} add(f32[24,2048]{1,0:T(8,128)} %get-tuple-element.5, f32[24,2048]{1,0:T(8,128)} %get-tuple-element.6) | non-fusion elementwise | flops 49152 | bytes 589824 | tf_op jit(solution)/shard_map/add | solution.py:416
  86.8 0.0 copy-done
  86.8 0.6 multiply_bitcast_fusion
Async XLA Ops:
  85.1 1.8 %copy-start = (f32[128,128]{1,0:T(8,128)S(1)}, f32[128,128]{1,0:T(8,128)}, u32[]{:S(2)}) copy-start(f32[128,128]{1,0:T(8,128)} %get-tuple-element.7) | copy-start | bytes 196612

commit v7 on v5

--- a/solution.py
+++ b/solution.py
@@ -74,7 +74,7 @@
 
 
 def kernel(
-    x_ref, target_ref, pairs_ref, owner_ref, big_ref, small_ref, margin_ref,
+    x_ref, target_ref, pairs_ref, owner_ref, out_ref, margin_ref,
     tabv, tab, hip_ref, tab_sem, oh_lo, masked, zout, zin, gdo, gdi, goo, goi, qd, qo, rdo, rdi, roo, roi, seg, zro, zri,
     mdo, mdi, mzo, mq, mko, moi, mall, mfo, mfi, upd, picked,
     ss, sr_z, sr_gd, sr_go, sr_qd, sr_qo, sr_rd, sr_ro, sr_zr, sr_md, sr_mz, sr_mq, sr_mo, sr_mf,
@@ -329,11 +329,12 @@
         for b in range(NBLK):
             zro[c][b] = seg[tab[T_LAST, b]]
         z_send(zro[c], zri[c], sr_zr.at[c], ss.at[21 + c])
+        if c == 0:
+            z_wait(mzo, mq.at[h], sr_mz, ss.at[6], 1).wait_recv()
+            q_send(mq, sr_mq, ss.at[0])
         zri[c][pl.ds(r * BPS, BPS)] = zro[c][pl.ds(r * BPS, BPS)]
         zri[c][NBLK] = zero
 
-    z_wait(mzo, mq.at[h], sr_mz, ss.at[6], 1).wait_recv()
-    q_send(mq, sr_mq, ss.at[0])
     c_wait(mko, moi, sr_mo, ss.at[8]).wait_recv()
     q_wait(mq, sr_mq, ss.at[0]).wait_recv()
     for b in range(NBLK):
@@ -354,11 +355,11 @@
             small = (u - big.astype(jnp.float32)).astype(jnp.bfloat16)
             upd[pl.ds(16 * t, 16), :] = jnp.concatenate([big, small], axis=0)
         picked[...] = jnp.dot(upd[...], oh_lo[...], preferred_element_type=jnp.float32)
-        for part, ref in enumerate((big_ref, small_ref)):
-            total = jnp.zeros((8, FD), jnp.float32)
-            for t in range(PACKED):
-                total = total + jnp.where(hip == t, picked[pl.ds(16 * t + 8 * part, 8), :], 0.0)
-            ref[pl.ds(8 * c, 8), :] = total
+        total = jnp.zeros((8, FD), jnp.float32)
+        for t in range(PACKED):
+            both = picked[pl.ds(16 * t, 8), :] + picked[pl.ds(16 * t + 8, 8), :]
+            total = total + jnp.where(hip == t, both, 0.0)
+        out_ref[pl.ds(8 * c, 8), :] = total
 
     c_wait(mfo, mfi, sr_mf, ss.at[11]).wait_recv()
     margin_ref[...] = mfi[...].reshape(FB, FB)
@@ -392,15 +393,14 @@
     z = [v((NBLK + 1, *tile), f32) for _ in range(NC)]
     pr = [v((NQ, 2, *tile), f32) for _ in range(NC)]
     un = v((NQ, 2, NC, *tile), f32)
-    big, small, margin = pl.pallas_call(
+    corrected, margin = pl.pallas_call(
         kernel,
         out_shape=(
-            jax.ShapeDtypeStruct((ROWS, FD), f32),
             jax.ShapeDtypeStruct((ROWS, FD), f32),
             jax.ShapeDtypeStruct((FB, FB), f32),
         ),
         in_specs=[vm, vm, vm, vm],
-        out_specs=(vm, vm, vm),
+        out_specs=(vm, vm),
         scratch_shapes=[
             v((8, FB), jnp.int32), pltpu.SMEM((8, FB), jnp.int32), v((1, FD), jnp.int32), dma,
             v((FB, FD), bf16), v((NBLK * 16, FD), bf16), z, z, un, un, pr, pr,
@@ -412,7 +412,7 @@
         ],
         compiler_params=pltpu.CompilerParams(collective_id=0, has_side_effects=True, vmem_limit_bytes=56 * 2**20),
     )(coeffs, region_of.reshape(1, FD), block_pairs[0].T, block_owner)
-    return big + small, (margin * (1.0 / COEFFICIENT_SIZE))[None, None]
+    return corrected, (margin * (1.0 / COEFFICIENT_SIZE))[None, None]
 
 
 def solution(mesh):

time: 87.4 us -> 88 us (level)
  local copies, waits for them, and re-layouts: 0.01 us -> 1.62 us
  other arithmetic: 2.39 us -> 1.48 us
    add x1 -> x0, other arithmetic: 1.75 us -> none  [body(): return (big + small, (margin * (1.0 / COEFFICIENT_SIZE))[None, None])]
    unnamed x2 -> x1, local copies, waits for them, and re-layouts: 0.01 us -> 1.62 us
where the time goes in v7:
time: 88 us; the launch traced here: 87.8 us
  Pallas kernels  84.1 us (96%)
  local copies, waits for them, and re-layouts  1.62 us (2%)
  other arithmetic  1.48 us (2%)
    pallas_call x1, Pallas kernels, body(): pl.pallas_call(kernel, out_shape=(jax.ShapeDtypeStruct((ROWS, FD), f32),...  84.1 us

profile of v7, /device:TPU:1, one launch (start us, length us, event | category | flops | bytes accessed | tf_op | source)
XLA Modules:
  0.0 87.8 jit_solution(10704541276114075382)
XLA Ops:
  0.6 84.1 %shard_map.59 = (f32[24,2048]{1,0:T(8,128)}, f32[128,128]{1,0:T(8,128)}) custom-call(f32[24,2048]{1,0:T(8,128)} %x_ref.1, s32[1,2048]{1,0:T(1,128)} %bitcast.6, s32[2,64]{1,0:T(2,128)} %bitcast.7, s32[1,64]{1,0:T(1,128)} %owner_ref.1), custom_call_target="tpu_custom_call" | custom-call | tf_op jit(solution)/shard_map/pallas_call | solution.py:396
  84.7 1.5 %multiply_bitcast_fusion = f32[1,1,128,128]{3,2,1,0:T(8,128)} fusion(f32[128,128]{1,0:T(8,128)} %get-tuple-element.5), kind=kLoop, calls=%fused_computation | loop fusion | flops 16384 | bytes 131072 | tf_op jit(solution)/shard_map/broadcast_in_dim | solution.py:415
  86.2 1.6 %copy.7 = f32[24,2048]{1,0:T(8,128)} copy(f32[24,2048]{1,0:T(8,128)} %get-tuple-element.8) | data formatting | bytes 393216
